TPU v7x, 32 devices: a whole 2x2x4 slice. The times are simulated.
32 devices in a mesh: seq: 8 (over z, y), head: 4 (over x, core).
Axes of the slice: x: 2, y: 2, z: 4, core: 2. Of those that a mesh axis runs over, the one named last changes fastest.
Arguments:
- queries: bfloat16 [4096, 4096], P(('seq', 'head')), may hold values from -52 to 52
- keys: bfloat16 [4096, 4096], P(('seq', 'head')), may hold values from -4 to 4
- values: bfloat16 [4096, 4096], P(('seq', 'head')), may hold values from -32 to 32
- grad_out: bfloat16 [4096, 4096], P(('seq', 'head')), may hold values from -64 to 64
- rand_blocks: int32 [32, 64, 3], P('head', 'seq'), may hold values from 0 to 63, as said below
- global_ids: int32 [2], replicated, may hold values from 0 to 63
- drop_mask: int32 [32, 64, 8], P('head', 'seq'), may hold values 0 or 1
Outputs:
- attended: bfloat16 [4096, 4096], P('seq', 'head')
- grad_queries: bfloat16 [4096, 4096], P('seq', 'head')
- grad_keys: bfloat16 [4096, 4096], P('seq', 'head')
- grad_values: bfloat16 [4096, 4096], P('seq', 'head')
Inputs may be any that keep to these rules, and one draw needn't show every extreme that they name: `rand_blocks`: for every sequence shard s (query blocks s * 8 onward) and head group g (heads g * 8 onward), the 192 listed random blocks come from a g-dependent hot shard exactly 30 times, and from no shard more than 30 times; the rest spread evenly over the other shards; the hot shard is the same for all s of one head group.
All inputs are finite; a program needn't handle non-finite values. No bound on the sum of `drop_mask` on one device may be relied on, other than what follows from the above.
Results may differ from a plain program's by a relative error of at most 0.015.
Values may be sent and summed in bfloat16 or wider, within the bound.
No kernel may reach another device: no remote copies, remote signals or barrier semaphores. Data moves between devices by JAX's collectives and lax.ppermute only.
A program may use at most 128 MiB of HBM per device.

v0:
```python
import jax
import jax.numpy as jnp
from jax import lax
from jax.sharding import PartitionSpec as P

HEAD_WIDTH = 128
BLOCK_TOKENS = 64
R = 3
G = 2


keep_prob = 0.9


def padded(block, sides, width):
    for axis, dim in sides:
        count = lax.axis_size(axis)
        forward = [(i, i + 1) for i in range(count - 1)]
        backward = [(target, source) for source, target in forward]
        low = lax.ppermute(
            lax.slice_in_dim(block, block.shape[dim] - width, None, axis=dim), axis, forward
        )
        high = lax.ppermute(lax.slice_in_dim(block, 0, width, axis=dim), axis, backward)
        block = jnp.concatenate([low, block, high], axis=dim)
    return block


def to_heads(tensor, head_count):
    return tensor.reshape(-1, BLOCK_TOKENS, head_count, HEAD_WIDTH).transpose(2, 0, 1, 3)


def to_tokens(tensor):
    head_count = tensor.shape[0]
    return tensor.transpose(1, 2, 0, 3).reshape(-1, head_count * HEAD_WIDTH)


def spread(terms):
    zeros_pad = ((0, 0), (0, 0), (0, 0))
    return (
        jnp.pad(terms[:, 0], ((0, 2),) + zeros_pad[1:])
        + jnp.pad(terms[:, 1], ((1, 1),) + zeros_pad[1:])
        + jnp.pad(terms[:, 2], ((2, 0),) + zeros_pad[1:])
    )


def per_device(queries, keys, values, grad_out, rand_blocks, global_ids, drop_mask):
    logit_scale = HEAD_WIDTH ** (-0.5)
    shard_count = lax.axis_size("seq")
    shard_index = lax.axis_index("seq")
    query_tok, key_tok, value_tok, grad_tok = (
        lax.all_to_all(queries, "head", split_axis=1, concat_axis=0, tiled=True),
        lax.all_to_all(keys, "head", split_axis=1, concat_axis=0, tiled=True),
        lax.all_to_all(values, "head", split_axis=1, concat_axis=0, tiled=True),
        lax.all_to_all(grad_out, "head", split_axis=1, concat_axis=0, tiled=True),
    )
    head_count = rand_blocks.shape[0]
    block_count = rand_blocks.shape[1]
    total_blocks = block_count * shard_count
    slot_total = 3 + G + R
    query_heads = to_heads(query_tok, head_count)
    grad_heads = to_heads(grad_tok, head_count)
    key_value = jnp.stack([to_heads(key_tok, head_count), to_heads(value_tok, head_count)])
    extended = padded(key_value, (("seq", 2),), 1)
    first_block = shard_index * block_count
    local_ids = global_ids - first_block
    is_owner = (local_ids >= 0) & (local_ids < block_count)
    local_ids = jnp.clip(local_ids, 0, block_count - 1)
    picked = key_value[:, :, local_ids].astype(jnp.float32) * is_owner[
        None, None, :, None, None
    ].astype(jnp.float32)
    global_kv = lax.psum(picked.astype(jnp.bfloat16), "seq")
    flat_ids = rand_blocks.reshape(-1)
    requests = flat_ids.shape[0]
    owners = flat_ids // block_count
    head_of = jnp.arange(requests, dtype=jnp.int32) // (block_count * R)
    tile_code = head_of * block_count + flat_ids % block_count
    capacity = 5 * requests // (4 * shard_count)
    shard_range = jnp.arange(shard_count, dtype=jnp.int32)
    onehot = (owners[:, None] == shard_range[None, :]).astype(jnp.int32)
    rank_of = jnp.sum((jnp.cumsum(onehot, axis=0) - onehot) * onehot, axis=1)
    slot_of = owners * capacity + rank_of
    request_table = (
        jnp.zeros((shard_count * capacity,), jnp.int32)
        .at[slot_of]
        .set(tile_code)
        .reshape(shard_count, capacity)
    )
    wanted = lax.all_to_all(request_table, "seq", split_axis=0, concat_axis=0, tiled=True)
    wanted_flat = wanted.reshape(-1)
    flat_pairs = key_value.reshape(2, head_count * block_count, BLOCK_TOKENS, HEAD_WIDTH)
    outgoing = flat_pairs[:, wanted_flat].reshape(
        2, shard_count, capacity, BLOCK_TOKENS, HEAD_WIDTH
    )
    arrived = lax.all_to_all(outgoing, "seq", split_axis=1, concat_axis=1, tiled=True)
    fetched = arrived.reshape(2, shard_count * capacity, BLOCK_TOKENS, HEAD_WIDTH)[
        :, slot_of
    ].reshape(2, head_count, block_count, R, BLOCK_TOKENS, HEAD_WIDTH)
    block_ids = first_block + jnp.arange(block_count, dtype=jnp.int32)
    present = jnp.concatenate(
        [
            (block_ids >= 1)[:, None],
            jnp.ones((block_count, 1), bool),
            (block_ids <= total_blocks - 2)[:, None],
            jnp.ones((block_count, G + R), bool),
        ],
        axis=1,
    )
    wide_present = jnp.repeat(present, BLOCK_TOKENS, axis=1)[:, None, :]
    split_position = (3 + G) * BLOCK_TOKENS

    def attend(inputs):
        query_lines, gradient_rows, ext_rows, global_rows, random_rows, drop_bits = inputs
        window_rows = jnp.stack([ext_rows[:, :-2], ext_rows[:, 1:-1], ext_rows[:, 2:]], axis=2)
        global_wide = jnp.broadcast_to(
            global_rows[:, None], (2, block_count, G, BLOCK_TOKENS, HEAD_WIDTH)
        )
        listed = jnp.concatenate([window_rows, global_wide, random_rows], axis=2).reshape(
            2, block_count, slot_total * BLOCK_TOKENS, HEAD_WIDTH
        )
        every_key = listed[0]
        every_value = listed[1]
        attention_logits = (
            jnp.einsum("ran,rln->ral", query_lines, every_key, preferred_element_type=jnp.float32)
            * logit_scale
        )
        attention_logits = jnp.where(wide_present, attention_logits, -jnp.inf)
        top_score = jnp.max(attention_logits, axis=-1, keepdims=True)
        expd = jnp.exp(attention_logits - top_score)
        probs = expd / jnp.sum(expd, axis=-1, keepdims=True)
        retain_scale = jnp.repeat(drop_bits.astype(jnp.float32) / keep_prob, BLOCK_TOKENS, axis=1)[
            :, None, :
        ]
        after_dropout = (probs * retain_scale).astype(jnp.bfloat16)
        attended = jnp.einsum(
            "ymn,ynh->ymh", after_dropout, every_value, preferred_element_type=jnp.float32
        ).astype(jnp.bfloat16)
        probability_grad = (
            jnp.einsum(
                "ran,rln->ral", gradient_rows, every_value, preferred_element_type=jnp.float32
            )
            * retain_scale
        )
        delta = jnp.sum(probs * probability_grad, axis=-1, keepdims=True)
        score_grad = (probs * (probability_grad - delta)).astype(jnp.bfloat16)
        query_gradient = (
            jnp.einsum("ymn,ynh->ymh", score_grad, every_key, preferred_element_type=jnp.float32)
            * logit_scale
        ).astype(jnp.bfloat16)
        key_main = (
            jnp.einsum(
                "efu,efy->euy",
                score_grad[:, :, :split_position],
                query_lines,
                preferred_element_type=jnp.float32,
            )
            * logit_scale
        ).reshape(block_count, 3 + G, BLOCK_TOKENS, HEAD_WIDTH)
        value_main = jnp.einsum(
            "efu,efy->euy",
            after_dropout[:, :, :split_position],
            gradient_rows,
            preferred_element_type=jnp.float32,
        ).reshape(block_count, 3 + G, BLOCK_TOKENS, HEAD_WIDTH)
        key_rand = (
            jnp.einsum(
                "efu,efy->euy",
                score_grad[:, :, split_position:],
                query_lines,
                preferred_element_type=jnp.float32,
            )
            * logit_scale
        ).reshape(block_count, R, BLOCK_TOKENS, HEAD_WIDTH)
        value_rand = jnp.einsum(
            "efu,efy->euy",
            after_dropout[:, :, split_position:],
            gradient_rows,
            preferred_element_type=jnp.float32,
        ).reshape(block_count, R, BLOCK_TOKENS, HEAD_WIDTH)
        window_sum = jnp.stack([spread(key_main), spread(value_main)])
        global_sum = jnp.stack(
            [jnp.sum(key_main[:, 3:], axis=0), jnp.sum(value_main[:, 3:], axis=0)]
        )
        random_terms = jnp.stack([key_rand, value_rand]).astype(jnp.bfloat16)
        score_rand = (
            score_grad[:, :, split_position:]
            .reshape(block_count, BLOCK_TOKENS, R, BLOCK_TOKENS)
            .transpose(0, 2, 1, 3)
        )
        drop_rand = (
            after_dropout[:, :, split_position:]
            .reshape(block_count, BLOCK_TOKENS, R, BLOCK_TOKENS)
            .transpose(0, 2, 1, 3)
        )
        factors = jnp.stack([score_rand, drop_rand])
        return (attended, query_gradient, window_sum, global_sum, random_terms, factors)

    attended, query_gradient, window_sum, global_sum, random_terms, factors = lax.map(
        attend,
        (
            query_heads,
            grad_heads,
            extended.transpose(1, 0, 2, 3, 4),
            global_kv.transpose(1, 0, 2, 3, 4),
            fetched.transpose(1, 0, 2, 3, 4, 5),
            drop_mask,
        ),
    )
    window_sum = window_sum.transpose(1, 0, 2, 3, 4)
    rim_terms = jnp.concatenate([window_sum[:, :, :1], window_sum[:, :, -1:]], axis=2)
    near_terms = padded(rim_terms.astype(jnp.bfloat16), (("seq", 2),), 1).astype(rim_terms.dtype)
    inner = window_sum[:, :, 1:-1]
    inner = inner.at[:, :, 0].add(near_terms[:, :, 0]).at[:, :, -1].add(near_terms[:, :, 3])
    global_total = lax.psum(global_sum.transpose(1, 0, 2, 3, 4).astype(jnp.bfloat16), "seq").astype(
        jnp.float32
    )
    inner = inner.at[:, :, local_ids].add(
        global_total * is_owner[None, None, :, None, None].astype(jnp.float32)
    )
    flat_inner = inner.reshape(2, head_count * block_count, BLOCK_TOKENS, HEAD_WIDTH)
    slot_terms = random_terms.transpose(1, 0, 2, 3, 4, 5).reshape(
        2, requests, BLOCK_TOKENS, HEAD_WIDTH
    )
    slot_buffer = (
        jnp.zeros((2, shard_count * capacity, BLOCK_TOKENS, HEAD_WIDTH), jnp.bfloat16)
        .at[:, slot_of]
        .set(slot_terms)
        .reshape(2, shard_count, capacity, BLOCK_TOKENS, HEAD_WIDTH)
    )
    returned = lax.all_to_all(slot_buffer, "seq", split_axis=1, concat_axis=1, tiled=True)
    flat_inner = flat_inner.at[:, wanted_flat].add(
        returned.reshape(2, shard_count * capacity, BLOCK_TOKENS, HEAD_WIDTH).astype(jnp.float32)
    )
    grads = flat_inner.reshape(2, head_count, block_count, BLOCK_TOKENS, HEAD_WIDTH).astype(
        jnp.bfloat16
    )
    return (
        to_tokens(attended),
        to_tokens(query_gradient),
        to_tokens(grads[0]),
        to_tokens(grads[1]),
    )


def solution(mesh):
    return jax.shard_map(
        per_device,
        mesh=mesh,
        in_specs=(
            P(("seq", "head"), None),
            P(("seq", "head"), None),
            P(("seq", "head"), None),
            P(("seq", "head"), None),
            P("head", "seq", None),
            P(),
            P("head", "seq", None),
        ),
        out_specs=(P("seq", "head"), P("seq", "head"), P("seq", "head"), P("seq", "head")),
        check_vma=False,
    )
```

profile of v0, /device:TPU:0, one launch (start us, length us, event | category | flops | bytes accessed | tf_op | source)
XLA Modules:
  0.0 821.4 jit_solution(2135533068317089379)
XLA Ops:
  11.3 7.3 all-to-all-start.3
  18.6 2.4 copy.234
  20.9 4.0 all-to-all-done.3
  24.9 3.5 all-to-all-start
  29.5 13.4 %all-to-all-done = bf16[128,4,1024]{2,0,1:T(8,128)(2,1)S(1)} async-done(((bf16[128,4,1024]{2,0,1:T(8,128)(2,1)}), bf16[128,4,1024]{2,0,1:T(8,128)(2,1)S(1)}, u32[]{:S(2)}, u32[]{:S(2)}) %all-to-all-start) | async-done | bytes 1048608 | tf_op jit(solution)/shard_map/all_to_all | solution.py:51
  42.9 3.5 all-to-all-start.1
  47.5 13.4 %all-to-all-done.1 = bf16[128,4,1024]{2,0,1:T(8,128)(2,1)S(1)} async-done(((bf16[128,4,1024]{2,0,1:T(8,128)(2,1)}), bf16[128,4,1024]{2,0,1:T(8,128)(2,1)S(1)}, u32[]{:S(2)}, u32[]{:S(2)}) %all-to-all-start.1) | async-done | bytes 1048608 | tf_op jit(solution)/shard_map/all_to_all | solution.py:52
  60.8 3.5 all-to-all-start.2
  64.4 2.3 copy.231
  67.9 10.9 %all-to-all-done.2 = bf16[128,4,1024]{2,0,1:T(8,128)(2,1)S(1)} async-done(((bf16[128,4,1024]{2,0,1:T(8,128)(2,1)}), bf16[128,4,1024]{2,0,1:T(8,128)(2,1)S(1)}, u32[]{:S(2)}, u32[]{:S(2)}) %all-to-all-start.2) | async-done | bytes 1048608 | tf_op jit(solution)/shard_map/all_to_all | solution.py:53
  78.8 4.3 all-to-all-start.5
  85.4 8.5 %gather_fusion.1 = bf16[240,2,64,128]{3,2,1,0:T(8,128)(2,1)} fusion(bf16[2,64,64,128]{3,2,1,0:T(8,128)(2,1)S(1)} %pad_maximum_fusion.1, s32[1024]{0:T(1024)S(1)} %pad_clamp_fusion.1), kind=kCustom, calls=%fused_computation.1 | custom fusion | bytes 15729600 | tf_op jit(solution)/shard_map/gather | solution.py:91
  93.9 9.2 %copy.164 = bf16[2,8,30,64,128]{4,3,2,0,1:T(8,128)(2,1)} copy(bf16[2,8,30,64,128]{4,3,0,2,1:T(8,128)(2,1)} %bitcast.318) | data formatting | bytes 15728640 | tf_op jit(solution)/shard_map/reshape | solution.py:91
  103.1 5.0 all-to-all-start.4
  109.9 1.6 pad_maximum_fusion
  111.4 3.0 gather_fusion
  114.4 2.1 fusion.42
  119.4 3.7 collective-permute-start
  126.0 55.6 %collective-permute-done = bf16[2,8,1,64,128]{4,3,2,1,0:T(8,128)(2,1)S(1)} collective-permute-done((bf16[2,8,1,64,128]{4,3,2,1,0:T(8,128)(2,1)S(1)}, bf16[2,8,1,64,128]{4,3,2,1,0:T(8,128)(2,1)S(1)}, u32[]{:S(2)}, u32[]{:S(2)}) %collective-permute-start) | collective-permute-done | bytes 262176 | tf_op jit(solution)/shard_map/ppermute | solution.py:20
  181.6 1.9 maximum_bitcast_fusion.3
  183.5 105.3 %all-to-all-done.4 = bf16[2,8,30,64,128]{4,3,2,0,1:T(8,128)(2,1)} async-done(((bf16[2,8,30,64,128]{4,3,2,0,1:T(8,128)(2,1)}), bf16[2,8,30,64,128]{4,3,2,0,1:T(8,128)(2,1)}, u32[]{:S(2)}, u32[]{:S(2)}) %all-to-all-start.4) | async-done | bytes 7864352 | tf_op jit(solution)/shard_map/all_to_all | solution.py:94
  288.8 9.0 %copy.165 = bf16[2,8,30,64,128]{4,3,2,1,0:T(8,128)(2,1)} copy(bf16[2,8,30,64,128]{4,3,2,0,1:T(8,128)(2,1)} %all-to-all-done.4) | data formatting | bytes 15728640 | tf_op jit(solution)/shard_map/all_to_all | solution.py:94
  297.8 11.3 %gather_fusion.2 = bf16[192,2,64,128]{3,2,1,0:T(8,128)(2,1)} fusion(bf16[2,240,64,128]{3,2,1,0:T(8,128)(2,1)} %bitcast.319, s32[1024]{0:T(1024)S(1)} %pad_clamp_fusion), kind=kCustom, calls=%fused_computation.2 | custom fusion | bytes 12583680 | tf_op jit(solution)/shard_map/gather | solution.py:95
  309.1 17.6 %all-reduce.10.cloned.1.call-done = bf16[8,2,2,64,128]{4,3,0,1,2:T(8,128)(2,1)} async-done(((bf16[8,2,2,64,128]{4,3,0,1,2:T(8,128)(2,1)}), bf16[8,2,2,64,128]{4,3,0,1,2:T(8,128)(2,1)}) %all-reduce.10.cloned.1.call-update) | async-done | bytes 524304 | tf_op jit(solution)/shard_map/psum | solution.py:71
  326.6 145.5 %while.23 = (s32[]{:T(128)}, bf16[8,8,64,128]{3,2,1,0:T(8,128)(2,1)}, bf16[8,8,64,128]{3,2,1,0:T(8,128)(2,1)}, f32[8,2,10,64,128]{4,3,2,0,1:T(8,128)}, bf16[8,2,...) while((s32[]{:T(128)}, ...), condition=%wide.region_11.12_spmd.clone, body=%wide.region_5.11_spmd.clone.sunk | while | flops 409862272 | bytes 35630088 | solution.py:197
  331.2 1.6 fusion.117
  349.4 1.6 fusion.117
  367.6 1.6 fusion.117
  403.9 1.6 fusion.117
  422.1 1.6 fusion.117
  440.3 1.6 fusion.117
  458.5 1.6 fusion.117
  472.1 7.7 copy.178
  479.8 5.2 broadcast_in_dim.114
  485.0 29.4 %scatter_fusion.1 = bf16[2,240,64,128]{3,2,1,0:T(8,128)(2,1)} fusion(bf16[2,240,64,128]{3,2,1,0:T(8,128)(2,1)} %broadcast_in_dim.114, s32[192]{0:T(256)S(1)} %bitcast.357, bf16[192,2,64,128]{3,2,1,0:T(8,128)(2,1)} %copy.178), kind=kCustom, calls=%fused_computation.5 | custom fusion | bytes 18875136 | tf_op jit(solution)/shard_map/scatter | solution.py:226
  514.4 8.9 %copy.179 = bf16[2,8,30,64,128]{4,3,2,0,1:T(8,128)(2,1)} copy(bf16[2,8,30,64,128]{4,3,2,1,0:T(8,128)(2,1)} %bitcast.315) | data formatting | bytes 15728640 | tf_op jit(solution)/shard_map/reshape | solution.py:227
  523.3 5.2 all-to-all-start.6
  528.5 3.2 bitcast_convert_fusion
  531.8 3.9 collective-permute-start.2
  540.9 4.7 slice.271
  545.7 54.7 %collective-permute-done.2 = bf16[2,8,1,64,128]{4,3,2,1,0:T(8,128)(2,1)S(1)} collective-permute-done((bf16[2,8,1,64,128]{4,3,2,1,0:T(8,128)(2,1)S(1)}, bf16[2,8,1,64,128]{4,3,2,1,0:T(8,128)(2,1)S(1)}, u32[]{:S(2)}, u32[]{:S(2)}) %collective-permute-start.2) | collective-permute-done | bytes 262176 | tf_op jit(solution)/shard_map/ppermute | solution.py:20
  600.4 1.9 fusion.44
  602.3 1.9 fusion.43
  604.2 140.1 %all-reduce.12.cloned.1.call-done = bf16[2,8,2,64,128]{4,3,2,0,1:T(8,128)(2,1)} async-done(((bf16[2,8,2,64,128]{4,3,2,0,1:T(8,128)(2,1)}), bf16[2,8,2,64,128]{4,3,2,0,1:T(8,128)(2,1)}) %all-reduce.12.cloned.1.call-update) | async-done | bytes 524304 | tf_op jit(solution)/shard_map/psum | solution.py:213
  745.5 2.9 scatter_fusion
  748.4 10.8 %copy.180 = f32[2,8,30,64,128]{4,3,0,2,1:T(8,128)} copy(bf16[2,8,30,64,128]{4,3,2,0,1:T(8,128)(2,1)} %all-to-all-done.6) | data formatting | bytes 23592960 | tf_op jit(solution)/shard_map/convert_element_type | solution.py:231
  759.2 48.6 %scatter_fusion.2 = f32[2,64,64,128]{3,2,1,0:T(8,128)} fusion(f32[2,64,64,128]{3,2,1,0:T(8,128)} %bitcast.32, s32[240]{0:T(256)S(1)} %bitcast.354, f32[240,2,64,128]{3,2,1,0:T(8,128)} %bitcast.314), kind=kCustom, calls=%fused_computation.6 | custom fusion | flops 3932160 | bytes 47186880 | tf_op jit(solution)/shard_map/scatter-add | solution.py:230
  807.8 2.7 convert_element_type.101
  (320 shorter events, 161.1 us)
Async XLA Ops:
  7.2 21.3 %copy-start.4 = (bf16[128,4096]{1,0:T(8,128)(2,1)S(1)}, bf16[128,4096]{1,0:T(8,128)(2,1)}, u32[]{:S(2)}) copy-start(bf16[128,4096]{1,0:T(8,128)(2,1)} %param.14) | copy-start | bytes 3145732
  11.3 13.7 %all-to-all-start.3 = ((s32[8,1,30]{2,1,0:T(1,128)}), s32[8,1,30]{2,1,0:T(1,128)S(1)}, u32[]{:S(2)}, u32[]{:S(2)}) async-start(s32[8,1,30]{2,1,0:T(1,128)} %all_to_all.69), calls=%async_computation.3 | async-start | bytes 8192 | tf_op jit(solution)/shard_map/all_to_all | solution.py:88
  18.5 27.9 %copy-start.5 = (bf16[128,4096]{1,0:T(8,128)(2,1)S(1)}, bf16[128,4096]{1,0:T(8,128)(2,1)}, u32[]{:S(2)}) copy-start(bf16[128,4096]{1,0:T(8,128)(2,1)} %param.15) | copy-start | bytes 3145732
  24.9 18.0 %all-to-all-start = ((bf16[128,4,1024]{2,0,1:T(8,128)(2,1)}), bf16[128,4,1024]{2,0,1:T(8,128)(2,1)S(1)}, u32[]{:S(2)}, u32[]{:S(2)}) async-start(bf16[128,4,1024]{2,0,1:T(8,128)(2,1)} %bitcast.231), calls=%async_computation | async-start | bytes 2097152 | tf_op jit(solution)/shard_map/all_to_all | solution.py:51
  42.9 23.8 %copy-start.1 = (bf16[128,4,1024]{2,0,1:T(8,128)(2,1)}, bf16[128,4,1024]{2,0,1:T(8,128)(2,1)S(1)}, u32[]{:S(2)}) copy-start(bf16[128,4,1024]{2,0,1:T(8,128)(2,1)S(1)} %all-to-all-done) | copy-start | bytes 3145732
  42.9 18.0 %all-to-all-start.1 = ((bf16[128,4,1024]{2,0,1:T(8,128)(2,1)}), bf16[128,4,1024]{2,0,1:T(8,128)(2,1)S(1)}, u32[]{:S(2)}, u32[]{:S(2)}) async-start(bf16[128,4,1024]{2,0,1:T(8,128)(2,1)} %bitcast.230), calls=%async_computation.1 | async-start | bytes 2097152 | tf_op jit(solution)/shard_map/all_to_all | solution.py:52
  60.8 18.0 %all-to-all-start.2 = ((bf16[128,4,1024]{2,0,1:T(8,128)(2,1)}), bf16[128,4,1024]{2,0,1:T(8,128)(2,1)S(1)}, u32[]{:S(2)}, u32[]{:S(2)}) async-start(bf16[128,4,1024]{2,0,1:T(8,128)(2,1)} %bitcast.327), calls=%async_computation.2 | async-start | bytes 2097152 | tf_op jit(solution)/shard_map/all_to_all | solution.py:53
  78.8 24.3 %all-to-all-start.5 = ((bf16[128,4,1024]{2,0,1:T(8,128)(2,1)}), bf16[128,4,1024]{2,0,1:T(8,128)(2,1)}, u32[]{:S(2)}, u32[]{:S(2)}) async-start(bf16[128,4,1024]{2,0,1:T(8,128)(2,1)} %bitcast.228), calls=%async_computation.5 | async-start | bytes 2097152 | tf_op jit(solution)/shard_map/all_to_all | solution.py:54
  103.1 5.3 copy-start.8
  103.1 5.5 copy-start.2
  103.1 6.7 copy-start
  103.1 185.6 %all-to-all-start.4 = ((bf16[2,8,30,64,128]{4,3,2,0,1:T(8,128)(2,1)}), bf16[2,8,30,64,128]{4,3,2,0,1:T(8,128)(2,1)}, u32[]{:S(2)}, u32[]{:S(2)}) async-start(bf16[2,8,30,64,128]{4,3,2,0,1:T(8,128)(2,1)} %copy.164), calls=%async_computation.4 | async-start | bytes 15728640 | tf_op jit(solution)/shard_map/all_to_all | solution.py:94
  108.2 218.4 %all-reduce.10.cloned.1.call-start = ((), (), s32[]{:S(2)}) async-start(), calls=%async_computation.7 | async-start | bytes 1048576 | tf_op jit(solution)/shard_map/psum | solution.py:71
  109.8 6.7 copy-start.3
  119.4 62.2 %collective-permute-start = (bf16[2,8,1,64,128]{4,3,2,1,0:T(8,128)(2,1)S(1)}, bf16[2,8,1,64,128]{4,3,2,1,0:T(8,128)(2,1)S(1)}, u32[]{:S(2)}, u32[]{:S(2)}) collective-permute-start(bf16[2,8,1,64,128]{4,3,2,1,0:T(8,128)(2,1)S(1)} %get-tuple-element.338), channel_id=1, source_target_pairs={{0,4},{4,8},{8,12},{12,16},{16,20},{20,24},{24,28},{1,5},{5,9},{9,... | collective-permute-start | bytes 786440 | tf_op jit(solution)/shard_map/ppermute | solution.py:20
  123.2 58.4 %collective-permute-start.1 = (bf16[2,8,1,64,128]{4,3,2,1,0:T(8,128)(2,1)S(1)}, bf16[2,8,1,64,128]{4,3,2,1,0:T(8,128)(2,1)S(1)}, u32[]{:S(2)}, u32[]{:S(2)}) collective-permute-start(bf16[2,8,1,64,128]{4,3,2,1,0:T(8,128)(2,1)S(1)} %get-tuple-element.339), channel_id=1, source_target_pairs={{4,0},{8,4},{12,8},{16,12},{20,16},{24,20},{28,24},{5,1},{9,5},{13... | collective-permute-start | bytes 786440 | tf_op jit(solution)/shard_map/ppermute | solution.py:23
  523.3 225.1 %all-to-all-start.6 = ((bf16[2,8,30,64,128]{4,3,2,0,1:T(8,128)(2,1)}), bf16[2,8,30,64,128]{4,3,2,0,1:T(8,128)(2,1)}, u32[]{:S(2)}, u32[]{:S(2)}) async-start(bf16[2,8,30,64,128]{4,3,2,0,1:T(8,128)(2,1)} %copy.179), calls=%async_computation.6 | async-start | bytes 15728640 | tf_op jit(solution)/shard_map/all_to_all | solution.py:229
  528.4 215.8 %all-reduce.12.cloned.1.call-start = ((), (), s32[]{:S(2)}) async-start(), calls=%async_computation.8 | async-start | bytes 1048576 | tf_op jit(solution)/shard_map/psum | solution.py:213
  528.5 8.5 %copy-start.7 = (bf16[8,8,64,128]{3,2,1,0:T(8,128)(2,1)S(1)}, bf16[8,8,64,128]{3,2,1,0:T(8,128)(2,1)}, u32[]{:S(2)}) copy-start(bf16[8,8,64,128]{3,2,1,0:T(8,128)(2,1)} %get-tuple-element.193) | copy-start | bytes 3145732
  531.7 7.2 copy-start.6
  531.8 68.6 %collective-permute-start.2 = (bf16[2,8,1,64,128]{4,3,2,1,0:T(8,128)(2,1)S(1)}, bf16[2,8,1,64,128]{4,3,2,1,0:T(8,128)(2,1)S(1)}, u32[]{:S(2)}, u32[]{:S(2)}) collective-permute-start(bf16[2,8,1,64,128]{4,3,2,1,0:T(8,128)(2,1)S(1)} %get-tuple-element.334), channel_id=1, source_target_pairs={{0,4},{4,8},{8,12},{12,16},{16,20},{20,24},{24,28},{1,5},{5,9},{9,... | collective-permute-start | bytes 786440 | tf_op jit(solution)/shard_map/ppermute | solution.py:20
  535.7 64.7 %collective-permute-start.3 = (bf16[2,8,1,64,128]{4,3,2,1,0:T(8,128)(2,1)S(1)}, bf16[2,8,1,64,128]{4,3,2,1,0:T(8,128)(2,1)S(1)}, u32[]{:S(2)}, u32[]{:S(2)}) collective-permute-start(bf16[2,8,1,64,128]{4,3,2,1,0:T(8,128)(2,1)S(1)} %get-tuple-element.335), channel_id=1, source_target_pairs={{4,0},{8,4},{12,8},{16,12},{20,16},{24,20},{28,24},{5,1},{9,5},{13... | collective-permute-start | bytes 786440 | tf_op jit(solution)/shard_map/ppermute | solution.py:23
Sparse Core Ops, SparseCore 0:
  116.6 209.9 all-reduce.9
  537.1 207.0 all-reduce.11
where the time goes:
time: 826 us; the launch traced here: 821 us
  waiting for transfers between devices  415 us (50%)
  local copies, waits for them, and re-layouts  166 us (20%)
  other arithmetic  99.6 us (12%)
  matrix products  82.7 us (10%)
  starting transfers between devices  42.8 us (5%)
  between operations  14.5 us (2%)
    psum x1, waiting for transfers between devices, per_device(): lax.psum(global_sum.transpose(1, 0, 2, 3, 4).astype(jnp.bfloat16), 'seq')  140 us
    ppermute x2, waiting for transfers between devices, padded(): lax.ppermute(lax.slice_in_dim(block, block.shape[dim] - width, None, axis...  110 us
    all_to_all x1, waiting for transfers between devices, per_device(): lax.all_to_all(outgoing, 'seq', split_axis=1, concat_axis=1, tiled=True)  105 us
    scatter-add x1, other arithmetic, per_device(): flat_inner.at[:, wanted_flat]  48.6 us
    scatter x1, local copies, waits for them, and re-layouts, per_device(): slot_buffer = jnp.zeros((2, shard_count * capacity, BLOCK_TOKENS, HEAD_WI...  29.4 us
    dynamic_update_slice x24, other arithmetic, per_device(): lax.map(attend, (query_heads, grad_heads, extended.transpose(1, 0, 2, 3,...  20.7 us
    psum x1, waiting for transfers between devices, per_device(): global_kv = lax.psum(picked.astype(jnp.bfloat16), 'seq')  17.6 us
  transfers between devices with their start and end apart: 13, of which 9 were waited for; matrix products, arithmetic and copies ran while one was open for 10% of the time, Pallas kernels for 0%

commit v1 on v0

v1 whole, which is shorter than its diff:
```python
import functools

import jax
import jax.numpy as jnp
from jax import lax
from jax.experimental import pallas as pl
from jax.experimental.pallas import tpu as pltpu
from jax.sharding import PartitionSpec as P

HEAD_WIDTH = 128
BLOCK_TOKENS = 64
R = 3
G = 2
SLOTS = 3 + G + R

keep_prob = 0.9


def attention_kernel(
    last_block,
    ids_ref,
    first_ref,
    drop_ref,
    q_ref,
    do_ref,
    k_ref,
    v_ref,
    att_ref,
    dq_ref,
    dk_ref,
    dv_ref,
    dk_acc,
    dv_acc,
    retain,
):
    scale = HEAD_WIDTH ** (-0.5)
    wide = SLOTS * BLOCK_TOKENS
    steps = drop_ref.shape[0]
    slot_of_lane = lax.broadcasted_iota(jnp.int32, (SLOTS, wide), 1) // BLOCK_TOKENS
    slot_row = lax.broadcasted_iota(jnp.int32, (SLOTS, wide), 0)
    expand = (slot_of_lane == slot_row).astype(jnp.float32)
    retain[...] = jnp.dot(
        drop_ref[...].astype(jnp.float32), expand, preferred_element_type=jnp.float32
    ) * (1.0 / keep_prob)
    dk_acc[...] = jnp.zeros_like(dk_acc)
    dv_acc[...] = jnp.zeros_like(dv_acc)
    lane = lax.broadcasted_iota(jnp.int32, (1, wide), 1)
    nt = (((1,), (1,)), ((), ()))
    tn = (((0,), (0,)), ((), ()))

    def one_block(j):
        rows = pl.ds(pl.multiple_of(j * BLOCK_TOKENS, BLOCK_TOKENS), BLOCK_TOKENS)
        places = [
            pl.ds(pl.multiple_of(ids_ref[j * SLOTS + s] * BLOCK_TOKENS, BLOCK_TOKENS), BLOCK_TOKENS)
            for s in range(SLOTS)
        ]
        block_id = first_ref[0] + j
        absent = ((block_id == 0) & (lane < BLOCK_TOKENS)) | (
            (block_id == last_block) & (lane >= 2 * BLOCK_TOKENS) & (lane < 3 * BLOCK_TOKENS)
        )
        q = q_ref[rows, :]
        do = do_ref[rows, :]
        keys = jnp.concatenate([k_ref[p, :] for p in places], axis=0)
        vals = jnp.concatenate([v_ref[p, :] for p in places], axis=0)
        logits = lax.dot_general(q, keys, nt, preferred_element_type=jnp.float32) * scale
        logits = jnp.where(absent, -jnp.inf, logits)
        top = jnp.max(logits, axis=-1, keepdims=True)
        expd = jnp.exp(logits - top)
        probs = expd * (1.0 / jnp.sum(expd, axis=-1, keepdims=True))
        keep = retain[pl.ds(j, 1), :]
        dropped = (probs * keep).astype(jnp.bfloat16)
        dprobs = lax.dot_general(do, vals, nt, preferred_element_type=jnp.float32) * keep
        delta = jnp.sum(probs * dprobs, axis=-1, keepdims=True)
        dscores = (probs * (dprobs - delta)).astype(jnp.bfloat16)
        att_ref[rows, :] = jnp.dot(dropped, vals, preferred_element_type=jnp.float32).astype(
            jnp.bfloat16
        )
        dq_ref[rows, :] = (
            jnp.dot(dscores, keys, preferred_element_type=jnp.float32) * scale
        ).astype(jnp.bfloat16)
        key_terms = lax.dot_general(dscores, q, tn, preferred_element_type=jnp.float32) * scale
        value_terms = lax.dot_general(dropped, do, tn, preferred_element_type=jnp.float32)
        for s, p in enumerate(places):
            part = slice(s * BLOCK_TOKENS, (s + 1) * BLOCK_TOKENS)
            dk_acc[p, :] += key_terms[part]
            dv_acc[p, :] += value_terms[part]

    def step(j, carry):
        one_block(j)
        return carry

    lax.fori_loop(0, steps, step, 0)
    dk_ref[...] = dk_acc[...].astype(dk_ref.dtype)
    dv_ref[...] = dv_acc[...].astype(dv_ref.dtype)


def attend(ids, first_block, drop, q, do, k, v, last_block, grad_type):
    steps = drop.shape[0]
    length = k.shape[0]
    vmem = pl.BlockSpec(memory_space=pltpu.VMEM)
    smem = pl.BlockSpec(memory_space=pltpu.SMEM)
    rows = q.shape
    pairs = steps * BLOCK_TOKENS * SLOTS * BLOCK_TOKENS
    return pl.pallas_call(
        functools.partial(attention_kernel, last_block),
        out_shape=(
            jax.ShapeDtypeStruct(rows, jnp.bfloat16),
            jax.ShapeDtypeStruct(rows, jnp.bfloat16),
            jax.ShapeDtypeStruct(k.shape, grad_type),
            jax.ShapeDtypeStruct(k.shape, grad_type),
        ),
        in_specs=[smem, smem, vmem, vmem, vmem, vmem, vmem],
        out_specs=(vmem, vmem, vmem, vmem),
        scratch_shapes=[
            pltpu.VMEM((length, HEAD_WIDTH), jnp.float32),
            pltpu.VMEM((length, HEAD_WIDTH), jnp.float32),
            pltpu.VMEM((steps, SLOTS * BLOCK_TOKENS), jnp.float32),
        ],
        compiler_params=pltpu.CompilerParams(vmem_limit_bytes=56 * 1024 * 1024),
        cost_estimate=pl.CostEstimate(
            flops=12 * pairs * HEAD_WIDTH,
            bytes_accessed=2 * (4 * q.size + 4 * k.size),
            transcendentals=pairs,
        ),
    )(ids, first_block, drop, q, do, k, v)


def per_device(queries, keys, values, grad_out, rand_blocks, global_ids, drop_mask):
    shards = lax.axis_size("seq")
    groups = lax.axis_size("head")
    shard = lax.axis_index("seq")
    heads, shard_blocks, _ = rand_blocks.shape
    tokens = queries.shape[0]
    teams = shards // heads
    team, member = shard // heads, shard % heads
    team_blocks = heads * shard_blocks
    total_blocks = shards * shard_blocks
    first_block = team * team_blocks
    whole = teams == 1
    same_team = None if whole else [[t * heads + m for m in range(heads)] for t in range(teams)]
    same_team_all = (
        None
        if whole
        else [
            [(t * heads + m) * groups + g for m in range(heads) for g in range(groups)]
            for t in range(teams)
        ]
    )
    same_head = [[t * heads + m for t in range(teams)] for m in range(heads)]

    tables = lax.all_gather(
        jnp.concatenate([rand_blocks, drop_mask], axis=2), "seq", axis=1, tiled=True
    )
    tables = lax.dynamic_slice(
        tables, (member, first_block, 0), (1, team_blocks, R + SLOTS)
    )[0]

    def by_head(tensor):
        return tensor.reshape(tokens, groups, heads, HEAD_WIDTH).transpose(2, 1, 0, 3)

    sent = jnp.stack([by_head(t) for t in (queries, keys, values, grad_out)], axis=2)
    sent = sent.reshape(heads * groups, 4, tokens, HEAD_WIDTH)
    got = lax.all_to_all(
        sent, ("seq", "head"), split_axis=0, concat_axis=0, tiled=True, axis_index_groups=same_team_all
    )
    q, k, v, do = [got[:, i].reshape(-1, HEAD_WIDTH) for i in range(4)]
    if not whole:
        k, v = [
            lax.all_gather(t, "seq", axis=0, tiled=True, axis_index_groups=same_head)
            for t in (k, v)
        ]
    blocks = first_block + jnp.arange(team_blocks, dtype=jnp.int32)
    window = jnp.stack([blocks - 1, blocks, blocks + 1], axis=1)
    listed = jnp.concatenate(
        [window, jnp.broadcast_to(global_ids[None], (team_blocks, G)), tables[:, :R]], axis=1
    )
    listed = jnp.clip(listed, 0, total_blocks - 1).reshape(-1)
    att, dq, dk, dv = attend(
        listed,
        first_block.reshape(1),
        tables[:, R:],
        q,
        do,
        k,
        v,
        total_blocks - 1,
        jnp.bfloat16 if whole else jnp.float32,
    )
    if not whole:
        dk, dv = [
            lax.psum_scatter(
                t, "seq", scatter_dimension=0, tiled=True, axis_index_groups=same_head
            ).astype(jnp.bfloat16)
            for t in (dk, dv)
        ]
    back = jnp.stack(
        [t.reshape(heads, groups * tokens, HEAD_WIDTH) for t in (att, dq, dk, dv)], axis=1
    )
    back = lax.all_to_all(
        back, "seq", split_axis=0, concat_axis=0, tiled=True, axis_index_groups=same_team
    )
    return tuple(
        back[:, i].transpose(1, 0, 2).reshape(groups * tokens, heads * HEAD_WIDTH)
        for i in range(4)
    )


def solution(mesh):
    return jax.shard_map(
        per_device,
        mesh=mesh,
        in_specs=(
            P(("seq", "head"), None),
            P(("seq", "head"), None),
            P(("seq", "head"), None),
            P(("seq", "head"), None),
            P("head", "seq", None),
            P(),
            P("head", "seq", None),
        ),
        out_specs=(P("seq", "head"), P("seq", "head"), P("seq", "head"), P("seq", "head")),
        check_vma=False,
    )
```

time: 826 us -> 288 us (0.35)
  waiting for transfers between devices: 415 us -> 0.01 us
  blocking collectives: 0 us -> 205 us
  local copies, waits for them, and re-layouts: 166 us -> 21 us
  other arithmetic: 99.6 us -> 4.78 us
  matrix products: 82.7 us -> 0 us
  Pallas kernels: 0 us -> 48.4 us
  starting transfers between devices: 42.8 us -> 7.43 us
  between operations: 14.5 us -> 0.84 us
    psum x2 -> x0, waiting for transfers between devices: 158 us -> none  [the longest x1 140 us: per_device(): lax.psum(global_sum.transpose(1, 0, 2, 3, 4).astype(jnp.bfloat16), 'seq')]
    all_to_all x7 -> x1, waiting for transfers between devices: 147 us -> 0.01 us  [per_device(): lax.all_to_all(sent, ('seq', 'head'), split_axis=0, concat_axis=0, tiled=...]
    all_gather x0 -> x1, blocking collectives: none -> 114 us  [per_device(): lax.all_gather(jnp.concatenate([rand_blocks, drop_mask], axis=2), 'seq',...]
    ppermute x4 -> x0, waiting for transfers between devices: 110 us -> none  [the longest x2 110 us: padded(): lax.ppermute(lax.slice_in_dim(block, block.shape[dim] - width, None, axis...]
    all_to_all x0 -> x1, blocking collectives: none -> 91 us  [per_device(): lax.all_to_all(back, 'seq', split_axis=0, concat_axis=0, tiled=True, axis...]
    dot_general x56 -> x0, matrix products: 70.2 us -> none  [the longest x8 11.8 us: attend(): jnp.einsum('ran,rln->ral', gradient_rows, every_value, preferred_element_...]
    scatter-add x4 -> x0, other arithmetic: 55.2 us -> none  [the longest x1 48.6 us: per_device(): flat_inner.at[:, wanted_flat]]
    pallas_call x0 -> x1, Pallas kernels: none -> 48.4 us  [attend(): pl.pallas_call(functools.partial(attention_kernel, last_block), out_shape...]
  transfers between devices with their start and end apart: 13 -> 1, of which waited for: 9 -> 0; matrix products, arithmetic and copies ran while one was open for 10% -> 1% of each run, Pallas kernels for 0% -> 0%
where the time goes in v1:
time: 288 us; the launch traced here: 287 us
  blocking collectives  205 us (71%)
  Pallas kernels  48.4 us (17%)
  local copies, waits for them, and re-layouts  21 us (7%)
  starting transfers between devices  7.43 us (3%)
  other arithmetic  4.78 us (2%)
    all_gather x1, blocking collectives, per_device(): lax.all_gather(jnp.concatenate([rand_blocks, drop_mask], axis=2), 'seq',...  114 us
    all_to_all x1, blocking collectives, per_device(): lax.all_to_all(back, 'seq', split_axis=0, concat_axis=0, tiled=True, axis...  91 us
    pallas_call x1, Pallas kernels, attend(): pl.pallas_call(functools.partial(attention_kernel, last_block), out_shape...  48.4 us
    unnamed x25, local copies, waits for them, and re-layouts  11.7 us
    all_to_all x1, starting transfers between devices, per_device(): lax.all_to_all(sent, ('seq', 'head'), split_axis=0, concat_axis=0, tiled=...  7.43 us
  transfers between devices with their start and end apart: 1, of which 0 were waited for; matrix products, arithmetic and copies ran while one was open for 1% of the time, Pallas kernels for 0%

profile of v1, /device:TPU:0, one launch (start us, length us, event | category | flops | bytes accessed | tf_op | source)
XLA Modules:
  0.0 287.4 jit_solution(2145875008633515958)
XLA Ops:
  0.6 0.0 copy-start
  0.6 0.0 copy-start.1
  0.7 1.6 copy.63
  2.2 0.4 copy.43
  2.7 0.0 copy-done
  2.7 0.0 copy-start.2
  2.7 0.2 copy.64
  2.9 0.4 copy.44
  3.4 0.0 copy-done.1
  3.4 0.2 copy.65
  3.6 0.4 copy.45
  4.0 0.0 copy-done.2
  4.0 0.2 copy.66
  4.3 0.4 copy.46
  4.7 2.2 pad_maximum_fusion
  7.0 0.0 copy-start.4
  7.0 0.0 copy-start.3
  7.0 0.0 copy-start.5
  7.0 7.4 %all-to-all-start = ((bf16[32,4,128,128]{3,2,1,0:T(8,128)(2,1)}), bf16[32,4,128,128]{3,2,1,0:T(8,128)(2,1)}, u32[]{:S(2)}, u32[]{:S(2)}) async-start(bf16[32,4,128,128]{3,2,1,0:T(8,128)(2,1)} %pad_maximum_fusion), calls=%async_computation | async-start | bytes 8388608 | tf_op jit(solution)/shard_map/all_to_all | solution.py:163
  14.4 0.0 copy-done.4
  14.4 0.1 copy.40
  14.6 0.0 copy-done.3
  14.6 0.1 pad_add_fusion
  14.6 113.8 %all_gather.3 = s32[8,64,11]{2,1,0:T(8,128)S(1)} all-gather(s32[8,8,11]{2,1,0:T(8,128)S(1)} %pad_add_fusion), channel_id=1, replica_groups=mesh['seq'=8,'head'=4] {'seq'}, dimensions={1}, use_global_device_ids=true | all-gather | bytes 25344 | tf_op jit(solution)/shard_map/all_gather | solution.py:151
  128.4 0.7 slice.41.drop_ref
  129.1 0.1 copy.41
  129.2 0.0 copy-done.5
  129.2 0.1 broadcast_in_dim.2
  129.3 0.1 copy.42
  129.4 0.7 min.12.ids_ref
  130.1 0.0 all-to-all-done
  130.1 4.4 %fusion.1 = (bf16[32,1,128,128]{3,2,1,0:T(8,128)(2,1)}, bf16[32,1,128,128]{3,2,1,0:T(8,128)(2,1)}, bf16[32,1,128,128]{3,2,1,0:T(8,128)(2,1)}, bf16[32,1,128,128]{3,2,1,0:T(8,128)(2,1)}) fusion(bf16[32,4,128,128]{3,2,1,0:T(8,128)(2,1)} %all-to-all-done), kind=kLoop, calls=%fused_computation.9 | loop fusion | bytes 8388608 | tf_op jit(solution)/shard_map/slice | solution.py:166
  134.5 48.4 %shard_map.102 = (bf16[4096,128]{1,0:T(8,128)(2,1)}, bf16[4096,128]{1,0:T(8,128)(2,1)}, bf16[4096,128]{1,0:T(8,128)(2,1)}, bf16[4096,128]{1,0:T(8,128)(2,1)}) custom-call(s32[512]{0:T(512)} %min.12.ids_ref, s32[1]{0:T(128)} %bitcast.1.first_ref, s32[64,8]{1,0:T(8,128)} %slice.41.drop_ref, bf16[4096,128]{1,0:T(8,128)(2,1)} %bitcast.83, ...), custom_call_target="tpu_custom_call" | custom-call | flops 3221225472 | bytes 8388608 | tf_op jit(solution)/shard_map/pallas_call | solution.py:104
  182.9 2.4 pad_maximum_fusion.1
  185.4 91.0 %all_to_all.10 = bf16[8,4,512,128]{3,2,1,0:T(8,128)(2,1)S(1)} all-to-all(bf16[8,4,512,128]{3,2,1,0:T(8,128)(2,1)S(1)} %pad_maximum_fusion.1), channel_id=1, replica_groups=mesh['seq'=8,'head'=4] {'seq'}, dimensions={0} | all-to-all | bytes 8388608 | tf_op jit(solution)/shard_map/all_to_all | solution.py:199
  276.4 1.7 fusion
  278.1 1.5 copy.62
  279.6 1.3 copy.58
  280.9 1.5 copy.61
  282.4 1.3 copy.57
  283.7 0.5 copy.60
  284.2 1.3 copy.56
  285.5 0.5 copy.59
  286.1 1.3 copy.55
  (5 shorter events, 0.0 us)
Async XLA Ops:
  0.6 2.0 copy-start
  0.6 2.7 copy-start.1
  2.7 1.4 copy-start.2
  7.0 7.5 %copy-start.4 = (s32[8,8,3]{1,0,2:T(8,128)S(1)}, s32[8,8,3]{1,0,2:T(8,128)}, u32[]{:S(2)}) copy-start(s32[8,8,3]{1,0,2:T(8,128)} %param.11) | copy-start | bytes 2308
  7.0 7.6 %copy-start.3 = (s32[8,8,8]{2,1,0:T(8,128)S(1)}, s32[8,8,8]{2,1,0:T(8,128)}, u32[]{:S(2)}) copy-start(s32[8,8,8]{2,1,0:T(8,128)} %param.13) | copy-start | bytes 6148
  7.0 122.3 %copy-start.5 = (s32[2]{0:T(128)S(1)}, s32[2]{0:T(128)}, u32[]{:S(2)}) copy-start(s32[2]{0:T(128)} %param.12) | copy-start | bytes 28
  7.0 123.1 %all-to-all-start = ((bf16[32,4,128,128]{3,2,1,0:T(8,128)(2,1)}), bf16[32,4,128,128]{3,2,1,0:T(8,128)(2,1)}, u32[]{:S(2)}, u32[]{:S(2)}) async-start(bf16[32,4,128,128]{3,2,1,0:T(8,128)(2,1)} %pad_maximum_fusion), calls=%async_computation | async-start | bytes 8388608 | tf_op jit(solution)/shard_map/all_to_all | solution.py:163

commit v2 on v1

v2 whole, which is shorter than its diff:
```python
import functools

import jax
import jax.numpy as jnp
from jax import lax
from jax.experimental import pallas as pl
from jax.experimental.pallas import tpu as pltpu
from jax.sharding import PartitionSpec as P

HEAD_WIDTH = 128
BLOCK_TOKENS = 64
R = 3
G = 2
SLOTS = 3 + G + R
VMEM_LIMIT = 56 * 1024 * 1024

keep_prob = 0.9

vmem = pl.BlockSpec(memory_space=pltpu.VMEM)
smem = pl.BlockSpec(memory_space=pltpu.SMEM)


def copy_cost(size):
    return pl.CostEstimate(flops=0, bytes_accessed=4 * size, transcendentals=0)


def pack_kernel(groups, heads, begin, *refs):
    sources, tables, out_ref = refs[:2], refs[2:-1], refs[-1]
    rows = (out_ref.shape[1] - (tables[0].shape[1] if tables else 0)) // 2
    for m in range(heads):
        for g in range(groups):
            columns = pl.ds((g * heads + m) * HEAD_WIDTH, HEAD_WIDTH)
            for n, ref in enumerate(sources):
                out_ref[m * groups + g, pl.ds(n * rows, rows), :] = ref[pl.ds(begin, rows), columns]
            for ref in tables:
                out_ref[m * groups + g, pl.ds(2 * rows, ref.shape[1]), :] = ref[m]


def pack(first, second, begin, rows, groups, heads, tables=()):
    extra = sum(t.shape[1] for t in tables)
    shape = (groups * heads, 2 * rows + extra, HEAD_WIDTH)
    return pl.pallas_call(
        functools.partial(pack_kernel, groups, heads, begin),
        out_shape=jax.ShapeDtypeStruct(shape, jnp.bfloat16),
        in_specs=[vmem] * (2 + len(tables)),
        out_specs=vmem,
        compiler_params=pltpu.CompilerParams(vmem_limit_bytes=VMEM_LIMIT),
        cost_estimate=copy_cost(shape[0] * shape[1] * shape[2]),
    )(first, second, *tables)


def unpack_kernel(device_blocks, *refs):
    pieces, outs = refs[:-2], refs[-2:]
    per = device_blocks // len(pieces)
    for c, piece in enumerate(pieces):
        heads, _, rows, _ = piece.shape
        run = per * BLOCK_TOKENS
        for n, out in enumerate(outs):
            for m in range(heads):
                for i in range(rows // run):
                    target = (i * device_blocks + c * per) * BLOCK_TOKENS
                    out[pl.ds(target, run), pl.ds(m * HEAD_WIDTH, HEAD_WIDTH)] = piece[
                        m, n, pl.ds(i * run, run), :
                    ]


def unpack(device_blocks, *pieces):
    heads = pieces[0].shape[0]
    rows = sum(p.shape[2] for p in pieces)
    shape = jax.ShapeDtypeStruct((rows, heads * HEAD_WIDTH), jnp.bfloat16)
    return pl.pallas_call(
        functools.partial(unpack_kernel, device_blocks),
        out_shape=(shape, shape),
        in_specs=[vmem] * len(pieces),
        out_specs=(vmem, vmem),
        compiler_params=pltpu.CompilerParams(vmem_limit_bytes=VMEM_LIMIT),
        cost_estimate=copy_cost(2 * rows * heads * HEAD_WIDTH),
    )(*pieces)


def attention_kernel(
    last_block, device_blocks, piece, has_start, is_last, ids_ref, first_ref, drop_ref, qd_ref, kv_ref, *refs
):
    refs = list(refs)
    starts = [refs.pop(0), refs.pop(0)] if has_start else None
    out_ref = refs.pop(0)
    if is_last:
        dkv_ref, dk_acc, dv_acc, retain = refs
    else:
        dk_acc, dv_acc, retain = refs
    scale = HEAD_WIDTH ** (-0.5)
    wide = SLOTS * BLOCK_TOKENS
    per = qd_ref.shape[1] // (2 * BLOCK_TOKENS)
    steps = qd_ref.shape[0] * per
    tokens = device_blocks * BLOCK_TOKENS
    slot_of_lane = lax.broadcasted_iota(jnp.int32, (SLOTS, wide), 1) // BLOCK_TOKENS
    slot_row = lax.broadcasted_iota(jnp.int32, (SLOTS, wide), 0)
    expand = (slot_of_lane == slot_row).astype(jnp.float32)
    retain[...] = jnp.dot(
        drop_ref[...].astype(jnp.float32), expand, preferred_element_type=jnp.float32
    ) * (1.0 / keep_prob)
    dk_acc[...] = starts[0][...] if has_start else jnp.zeros_like(dk_acc)
    dv_acc[...] = starts[1][...] if has_start else jnp.zeros_like(dv_acc)
    lane = lax.broadcasted_iota(jnp.int32, (1, wide), 1)
    nt = (((1,), (1,)), ((), ()))
    tn = (((0,), (0,)), ((), ()))
    out_steps = steps // out_ref.shape[0]

    def block_rows(number):
        return pl.ds(pl.multiple_of(number * BLOCK_TOKENS, BLOCK_TOKENS), BLOCK_TOKENS)

    def one_block(i):
        source, sub = i // per, i % per
        j = source * device_blocks + piece * per + sub
        ids = [ids_ref[j * SLOTS + s] for s in range(SLOTS)]
        places = [block_rows(b) for b in ids]
        block_id = first_ref[0] + j
        absent = ((block_id == 0) & (lane < BLOCK_TOKENS)) | (
            (block_id == last_block) & (lane >= 2 * BLOCK_TOKENS) & (lane < 3 * BLOCK_TOKENS)
        )
        q = qd_ref[source, block_rows(sub), :]
        do = qd_ref[source, block_rows(per + sub), :]
        keys = jnp.concatenate(
            [kv_ref[b // device_blocks, block_rows(b % device_blocks), :] for b in ids], axis=0
        )
        vals = jnp.concatenate(
            [
                kv_ref[b // device_blocks, block_rows(device_blocks + b % device_blocks), :]
                for b in ids
            ],
            axis=0,
        )
        logits = lax.dot_general(q, keys, nt, preferred_element_type=jnp.float32) * scale
        logits = jnp.where(absent, -jnp.inf, logits)
        top = jnp.max(logits, axis=-1, keepdims=True)
        expd = jnp.exp(logits - top)
        probs = expd * (1.0 / jnp.sum(expd, axis=-1, keepdims=True))
        keep = retain[pl.ds(j, 1), :]
        dropped = (probs * keep).astype(jnp.bfloat16)
        dprobs = lax.dot_general(do, vals, nt, preferred_element_type=jnp.float32) * keep
        delta = jnp.sum(probs * dprobs, axis=-1, keepdims=True)
        dscores = (probs * (dprobs - delta)).astype(jnp.bfloat16)
        target, pos = i // out_steps, i % out_steps
        out_ref[target, 0, block_rows(pos), :] = jnp.dot(
            dropped, vals, preferred_element_type=jnp.float32
        ).astype(jnp.bfloat16)
        out_ref[target, 1, block_rows(pos), :] = (
            jnp.dot(dscores, keys, preferred_element_type=jnp.float32) * scale
        ).astype(jnp.bfloat16)
        key_terms = lax.dot_general(dscores, q, tn, preferred_element_type=jnp.float32) * scale
        value_terms = lax.dot_general(dropped, do, tn, preferred_element_type=jnp.float32)
        return places, key_terms, value_terms

    def step(i, carry):
        done = [one_block(2 * i), one_block(2 * i + 1)]
        for places, key_terms, value_terms in done:
            for s, p in enumerate(places):
                part = slice(s * BLOCK_TOKENS, (s + 1) * BLOCK_TOKENS)
                dk_acc[p, :] += key_terms[part]
                dv_acc[p, :] += value_terms[part]
        return carry

    lax.fori_loop(0, steps // 2, step, 0)
    if is_last:
        shards, _, rows, _ = dkv_ref.shape
        for s in range(shards):
            dkv_ref[s, 0] = dk_acc[pl.ds(s * rows, rows), :].astype(dkv_ref.dtype)
            dkv_ref[s, 1] = dv_acc[pl.ds(s * rows, rows), :].astype(dkv_ref.dtype)


def attend(ids, first_block, drop, qd, kv, starts, piece, is_last, device_blocks, total_blocks, shards, targets, grad_type):
    team_blocks = drop.shape[0]
    steps = qd.shape[0] * qd.shape[1] // (2 * BLOCK_TOKENS)
    length = total_blocks * BLOCK_TOKENS
    pairs = steps * BLOCK_TOKENS * SLOTS * BLOCK_TOKENS
    accumulator = (length, HEAD_WIDTH)
    out_shape = [
        jax.ShapeDtypeStruct((targets, 2, steps * BLOCK_TOKENS // targets, HEAD_WIDTH), jnp.bfloat16)
    ]
    scratch = [pltpu.VMEM((team_blocks, SLOTS * BLOCK_TOKENS), jnp.float32)]
    if is_last:
        out_shape.append(
            jax.ShapeDtypeStruct((shards, 2, length // shards, HEAD_WIDTH), grad_type)
        )
        scratch = [pltpu.VMEM(accumulator, jnp.float32)] * 2 + scratch
    else:
        out_shape += [jax.ShapeDtypeStruct(accumulator, jnp.float32)] * 2
    return pl.pallas_call(
        functools.partial(
            attention_kernel, total_blocks - 1, device_blocks, piece, bool(starts), is_last
        ),
        out_shape=out_shape,
        in_specs=[smem, smem] + [vmem] * (3 + len(starts)),
        out_specs=[vmem] * len(out_shape),
        scratch_shapes=scratch,
        compiler_params=pltpu.CompilerParams(vmem_limit_bytes=VMEM_LIMIT),
        cost_estimate=pl.CostEstimate(
            flops=12 * pairs * HEAD_WIDTH,
            bytes_accessed=2 * (2 * qd.size + kv.size) + 8 * length * HEAD_WIDTH,
            transcendentals=pairs,
        ),
    )(ids, first_block, drop, qd, kv, *starts)


def per_device(queries, keys, values, grad_out, rand_blocks, global_ids, drop_mask):
    shards = lax.axis_size("seq")
    groups = lax.axis_size("head")
    shard = lax.axis_index("seq")
    heads, shard_blocks, _ = rand_blocks.shape
    tokens = queries.shape[0]
    device_blocks = tokens // BLOCK_TOKENS
    teams = shards // heads
    team = shard // heads
    team_blocks = heads * shard_blocks
    total_blocks = shards * shard_blocks
    first_block = team * team_blocks
    whole = teams == 1
    pieces = device_blocks if whole else 1
    rows = tokens // pieces
    same_team = None if whole else [[t * heads + m for m in range(heads)] for t in range(teams)]
    same_team_all = (
        None
        if whole
        else [
            [(t * heads + m) * groups + g for m in range(heads) for g in range(groups)]
            for t in range(teams)
        ]
    )
    same_head = [[t * heads + m for t in range(teams)] for m in range(heads)]

    def to_heads(packed):
        return lax.all_to_all(
            packed,
            ("seq", "head"),
            split_axis=0,
            concat_axis=0,
            tiled=True,
            axis_index_groups=same_team_all,
        )

    def to_shards(results):
        return lax.all_to_all(
            results, "seq", split_axis=0, concat_axis=0, tiled=True, axis_index_groups=same_team
        )

    table_rows = -(-shard_blocks // 16) * 16
    tables = jnp.concatenate([rand_blocks, drop_mask], axis=2).astype(jnp.bfloat16)
    tables = jnp.pad(
        tables, ((0, 0), (0, table_rows - shard_blocks), (0, HEAD_WIDTH - R - SLOTS))
    )
    kv = to_heads(pack(keys, values, 0, tokens, groups, heads, (tables,)))
    qd = [
        to_heads(pack(queries, grad_out, c * rows, rows, groups, heads)) for c in range(pieces)
    ]
    tables = lax.dynamic_index_in_dim(
        kv.reshape(heads, groups, -1, HEAD_WIDTH)[
            :, :, 2 * tokens : 2 * tokens + shard_blocks, : R + SLOTS
        ],
        lax.axis_index("head"),
        axis=1,
        keepdims=False,
    )
    tables = tables.reshape(team_blocks, R + SLOTS).astype(jnp.int32)
    if not whole:
        kv = lax.all_gather(kv, "seq", axis=0, tiled=True, axis_index_groups=same_head)
    blocks = first_block + jnp.arange(team_blocks, dtype=jnp.int32)
    window = jnp.stack([blocks - 1, blocks, blocks + 1], axis=1)
    listed = jnp.concatenate(
        [window, jnp.broadcast_to(global_ids[None], (team_blocks, G)), tables[:, :R]], axis=1
    )
    listed = jnp.clip(listed, 0, total_blocks - 1).reshape(-1)
    near, sums = [], ()
    for c in range(pieces):
        result, *sums = attend(
            listed,
            first_block.reshape(1),
            tables[:, R:],
            qd[c],
            kv,
            sums,
            c,
            c == pieces - 1,
            device_blocks,
            total_blocks,
            shards,
            heads,
            jnp.bfloat16 if whole else jnp.float32,
        )
        near.append(to_shards(result))
    grads = sums[0]
    if not whole:
        grads = lax.psum_scatter(
            grads, "seq", scatter_dimension=0, tiled=True, axis_index_groups=same_head
        ).astype(jnp.bfloat16)
    grads = to_shards(grads)
    return (*unpack(device_blocks, *near), *unpack(device_blocks, grads))


def solution(mesh):
    return jax.shard_map(
        per_device,
        mesh=mesh,
        in_specs=(
            P(("seq", "head"), None),
            P(("seq", "head"), None),
            P(("seq", "head"), None),
            P(("seq", "head"), None),
            P("head", "seq", None),
            P(),
            P("head", "seq", None),
        ),
        out_specs=(P("seq", "head"), P("seq", "head"), P("seq", "head"), P("seq", "head")),
        check_vma=False,
    )
```

time: 288 us -> 245 us (0.85)
  blocking collectives: 205 us -> 31.4 us
  waiting for transfers between devices: 0.01 us -> 116 us
  Pallas kernels: 48.4 us -> 66.7 us
  starting transfers between devices: 7.43 us -> 24.3 us
  local copies, waits for them, and re-layouts: 21 us -> 5.07 us
  other arithmetic: 4.78 us -> 0.74 us
    all_to_all x1 -> x5, waiting for transfers between devices: 0.01 us -> 116 us  [the longest x3 71 us: to_heads(): lax.all_to_all(packed, ('seq', 'head'), split_axis=0, concat_axis=0, tile...]
    all_gather x1 -> x0, blocking collectives: 114 us -> none  [per_device(): lax.all_gather(jnp.concatenate([rand_blocks, drop_mask], axis=2), 'seq',...]
    all_to_all x1, blocking collectives: 91 us -> 31.4 us  [to_shards(): lax.all_to_all(results, 'seq', split_axis=0, concat_axis=0, tiled=True, a...]
    pallas_call x1 -> x7, Pallas kernels: 48.4 us -> 66.7 us  [the longest x2 51 us: attend(): pl.pallas_call(functools.partial(attention_kernel, total_blocks - 1, devi...]
    all_to_all x1 -> x5, starting transfers between devices: 7.43 us -> 24.3 us  [the longest x3 14.9 us: to_heads(): lax.all_to_all(packed, ('seq', 'head'), split_axis=0, concat_axis=0, tile...]
    unnamed x25 -> x16, local copies, waits for them, and re-layouts: 11.7 us -> 3.29 us
    slice x2 -> x1, local copies, waits for them, and re-layouts: 6.06 us -> 0.01 us  [per_device(): kv.reshape(heads, groups, -1, HEAD_WIDTH)]
    another operation x2, other arithmetic: 4.69 us -> 0.01 us  [the longest x1 2.44 us: per_device(): jnp.stack([t.reshape(heads, groups * tokens, HEAD_WIDTH) for t in (att, d...]
  transfers between devices with their start and end apart: 1 -> 5, of which waited for: 0 -> 4; matrix products, arithmetic and copies ran while one was open for 1% -> 1% of each run, Pallas kernels for 0% -> 25%
where the time goes in v2:
time: 245 us
  waiting for transfers between devices  116 us (47%)
  Pallas kernels  66.7 us (27%)
  blocking collectives  31.4 us (13%)
  starting transfers between devices  24.3 us (10%)
  local copies, waits for them, and re-layouts  5.07 us (2%)
    all_to_all x3, waiting for transfers between devices, to_heads(): lax.all_to_all(packed, ('seq', 'head'), split_axis=0, concat_axis=0, tile...  71 us
    pallas_call x2, Pallas kernels, attend(): pl.pallas_call(functools.partial(attention_kernel, total_blocks - 1, devi...  51 us
    all_to_all x2, waiting for transfers between devices, to_shards(): lax.all_to_all(results, 'seq', split_axis=0, concat_axis=0, tiled=True, a...  44.6 us
    all_to_all x1, blocking collectives, to_shards(): lax.all_to_all(results, 'seq', split_axis=0, concat_axis=0, tiled=True, a...  31.4 us
    all_to_all x3, starting transfers between devices, to_heads(): lax.all_to_all(packed, ('seq', 'head'), split_axis=0, concat_axis=0, tile...  14.9 us
    all_to_all x2, starting transfers between devices, to_shards(): lax.all_to_all(results, 'seq', split_axis=0, concat_axis=0, tiled=True, a...  9.41 us
    pallas_call x3, Pallas kernels, pack(): pl.pallas_call(functools.partial(pack_kernel, groups, heads, begin), out_...  8.79 us
    pallas_call x2, Pallas kernels, unpack(): pl.pallas_call(functools.partial(unpack_kernel, device_blocks), out_shape...  6.94 us
  transfers between devices with their start and end apart: 5, of which 4 were waited for; matrix products, arithmetic and copies ran while one was open for 1% of the time, Pallas kernels for 25%

profile of v2, /device:TPU:0, one launch (start us, length us, event | category | flops | bytes accessed | tf_op | source)
XLA Modules:
  0.0 244.7 jit_solution(3590185788257173484)
XLA Ops:
  0.6 0.0 copy-start.5
  0.6 0.0 copy-start.6
  0.7 2.7 %shard_map.103 = bf16[32,128,128]{2,1,0:T(8,128)(2,1)} custom-call(bf16[128,4096]{1,0:T(8,128)(2,1)} %refs_0_.5, bf16[128,4096]{1,0:T(8,128)(2,1)} %refs_1_.5), custom_call_target="tpu_custom_call" | custom-call | bytes 2097152 | tf_op jit(solution)/shard_map/pallas_call | solution.py:42
  3.4 7.3 %all-to-all-start.1 = ((bf16[32,128,128]{2,1,0:T(8,128)(2,1)}), bf16[32,128,128]{2,1,0:T(8,128)(2,1)S(1)}, u32[]{:S(2)}, u32[]{:S(2)}) async-start(bf16[32,128,128]{2,1,0:T(8,128)(2,1)} %shard_map.103), calls=%async_computation.1 | async-start | bytes 2097152 | tf_op jit(solution)/shard_map/all_to_all | solution.py:232
  10.7 0.0 copy-done.5
  10.7 0.0 copy-done.6
  10.7 0.1 copy.16
  10.8 0.7 fusion.5.refs_2_
  11.5 3.4 %shard_map.102 = bf16[32,272,128]{2,1,0:T(8,128)(2,1)} custom-call(bf16[128,4096]{1,0:T(8,128)(2,1)} %refs_0_.3, bf16[128,4096]{1,0:T(8,128)(2,1)} %refs_1_.3, bf16[8,16,128]{2,1,0:T(8,128)(2,1)} %fusion.5.refs_2_), custom_call_target="tpu_custom_call" | custom-call | bytes 4456448 | tf_op jit(solution)/shard_map/pallas_call | solution.py:42
  14.9 22.0 %all-to-all-done.1.qd_ref = bf16[32,128,128]{2,1,0:T(8,128)(2,1)S(1)} async-done(((bf16[32,128,128]{2,1,0:T(8,128)(2,1)}), bf16[32,128,128]{2,1,0:T(8,128)(2,1)S(1)}, u32[]{:S(2)}, u32[]{:S(2)}) %all-to-all-start.1) | async-done | bytes 1048608 | tf_op jit(solution)/shard_map/all_to_all | solution.py:232
  36.9 0.0 copy-start.4
  36.9 1.0 copy-done.4
  37.9 3.6 %all-to-all-start = ((bf16[32,272,128]{2,1,0:T(8,128)(2,1)}), bf16[32,272,128]{2,1,0:T(8,128)(2,1)S(1)}, u32[]{:S(2)}, u32[]{:S(2)}) async-start(bf16[32,272,128]{2,1,0:T(8,128)(2,1)} %shard_map.102), calls=%async_computation | async-start | bytes 4456448 | tf_op jit(solution)/shard_map/all_to_all | solution.py:232
  41.5 0.0 copy-start.7
  41.5 2.7 %shard_map.105 = bf16[32,128,128]{2,1,0:T(8,128)(2,1)} custom-call(bf16[128,4096]{1,0:T(8,128)(2,1)} %refs_0_.5, bf16[128,4096]{1,0:T(8,128)(2,1)} %refs_1_.5), custom_call_target="tpu_custom_call" | custom-call | bytes 2097152 | tf_op jit(solution)/shard_map/pallas_call | solution.py:42
  44.2 49.0 %all-to-all-done.kv_ref = bf16[32,272,128]{2,1,0:T(8,128)(2,1)S(1)} async-done(((bf16[32,272,128]{2,1,0:T(8,128)(2,1)}), bf16[32,272,128]{2,1,0:T(8,128)(2,1)S(1)}, u32[]{:S(2)}, u32[]{:S(2)}) %all-to-all-start) | async-done | bytes 2228256 | tf_op jit(solution)/shard_map/all_to_all | solution.py:232
  93.2 0.0 copy-start
  93.2 4.0 %all-to-all-start.3 = ((bf16[32,128,128]{2,1,0:T(8,128)(2,1)}), bf16[32,128,128]{2,1,0:T(8,128)(2,1)S(1)}, u32[]{:S(2)}, u32[]{:S(2)}) async-start(bf16[32,128,128]{2,1,0:T(8,128)(2,1)} %shard_map.105), calls=%async_computation.3 | async-start | bytes 2097152 | tf_op jit(solution)/shard_map/all_to_all | solution.py:232
  97.3 0.7 slice.15.drop_ref
  98.0 0.1 copy.17
  98.1 0.0 copy-done.7
  98.1 0.1 broadcast_in_dim.2
  98.2 0.1 copy.18
  98.3 0.7 min.12.ids_ref
  99.0 0.0 copy-done
  99.0 25.2 %shard_map.104 = (bf16[8,2,256,128]{3,2,1,0:T(8,128)(2,1)}, f32[4096,128]{1,0:T(8,128)}, f32[4096,128]{1,0:T(8,128)}) custom-call(s32[512]{0:T(512)} %min.12.ids_ref, s32[1]{0:T(128)} %bitcast.2.first_ref, s32[64,8]{1,0:T(8,128)} %slice.15.drop_ref, bf16[32,128,128]{2,1,0:T(8,128)(2,1)} %copy-done.4, bf16[32,272,128]{2,1,0:T(8,128)(2,1)} %copy-done), custom_call_target="tpu_custom_call" | custom-call | flops 1610612736 | bytes 8519680 | tf_op jit(solution)/shard_map/pallas_call | solution.py:188
  124.2 0.0 all-to-all-done.3.qd_ref
  124.2 0.0 copy-start.3
  124.2 1.0 copy-done.3
  125.1 5.8 %all-to-all-start.2 = ((bf16[8,2,256,128]{3,2,1,0:T(8,128)(2,1)}), bf16[8,2,256,128]{3,2,1,0:T(8,128)(2,1)S(1)}, u32[]{:S(2)}, u32[]{:S(2)}) async-start(bf16[8,2,256,128]{3,2,1,0:T(8,128)(2,1)} %get-tuple-element.13), calls=%async_computation.2 | async-start | bytes 2097152 | tf_op jit(solution)/shard_map/all_to_all | solution.py:242
  130.9 25.8 %shard_map.106 = (bf16[8,2,256,128]{3,2,1,0:T(8,128)(2,1)}, bf16[8,2,512,128]{3,2,1,0:T(8,128)(2,1)}) custom-call(s32[512]{0:T(512)} %min.12.ids_ref, s32[1]{0:T(128)} %bitcast.2.first_ref, s32[64,8]{1,0:T(8,128)} %slice.15.drop_ref, bf16[32,128,128]{2,1,0:T(8,128)(2,1)} %copy-done.3, bf16[32,272,128]{2,1,0:T(8,128)(2,1)} %copy-done, ...), custom_call_target="tpu_custom_call" | custom-call | flops 1610612736 | bytes 8519680 | tf_op jit(solution)/shard_map/pallas_call | solution.py:188
  156.8 0.3 all-to-all-done.2.refs_0_
  157.0 0.0 copy-start.2
  157.0 31.4 %all_to_all.30.refs_1_ = bf16[8,2,256,128]{3,2,1,0:T(8,128)(2,1)} all-to-all(bf16[8,2,256,128]{3,2,1,0:T(8,128)(2,1)} %get-tuple-element.16), channel_id=1, replica_groups=mesh['seq'=8,'head'=4] {'seq'}, dimensions={0} | all-to-all | bytes 2097152 | tf_op jit(solution)/shard_map/all_to_all | solution.py:242
  188.5 0.0 copy-done.2
  188.5 3.6 %all-to-all-start.5 = ((bf16[8,2,512,128]{3,2,1,0:T(8,128)(2,1)}), bf16[8,2,512,128]{3,2,1,0:T(8,128)(2,1)S(1)}, u32[]{:S(2)}, u32[]{:S(2)}) async-start(bf16[8,2,512,128]{3,2,1,0:T(8,128)(2,1)} %get-tuple-element.19), calls=%async_computation.5 | async-start | bytes 4194304 | tf_op jit(solution)/shard_map/all_to_all | solution.py:242
  192.1 3.4 %shard_map.107 = (bf16[512,1024]{1,0:T(8,128)(2,1)}, bf16[512,1024]{1,0:T(8,128)(2,1)}) custom-call(bf16[8,2,256,128]{3,2,1,0:T(8,128)(2,1)} %copy-done.2, bf16[8,2,256,128]{3,2,1,0:T(8,128)(2,1)} %all_to_all.30.refs_1_), custom_call_target="tpu_custom_call" | custom-call | bytes 4194304 | tf_op jit(solution)/shard_map/pallas_call | solution.py:71
  195.5 44.4 %all-to-all-done.5.refs_0_ = bf16[8,2,512,128]{3,2,1,0:T(8,128)(2,1)S(1)} async-done(((bf16[8,2,512,128]{3,2,1,0:T(8,128)(2,1)}), bf16[8,2,512,128]{3,2,1,0:T(8,128)(2,1)S(1)}, u32[]{:S(2)}, u32[]{:S(2)}) %all-to-all-start.5) | async-done | bytes 2097184 | tf_op jit(solution)/shard_map/all_to_all | solution.py:242
  239.9 0.0 copy-start.1
  239.9 1.3 copy-done.1
  241.2 3.5 %shard_map.108 = (bf16[512,1024]{1,0:T(8,128)(2,1)}, bf16[512,1024]{1,0:T(8,128)(2,1)}) custom-call(bf16[8,2,512,128]{3,2,1,0:T(8,128)(2,1)} %copy-done.1), custom_call_target="tpu_custom_call" | custom-call | bytes 4194304 | tf_op jit(solution)/shard_map/pallas_call | solution.py:71
  (8 shorter events, 0.1 us)
Async XLA Ops:
  0.6 10.0 %copy-start.5 = (s32[8,8,8]{2,1,0:T(8,128)S(1)}, s32[8,8,8]{2,1,0:T(8,128)}, u32[]{:S(2)}) copy-start(s32[8,8,8]{2,1,0:T(8,128)} %param.13) | copy-start | bytes 6148
  0.6 10.1 %copy-start.6 = (s32[8,8,3]{1,0,2:T(8,128)S(1)}, s32[8,8,3]{1,0,2:T(8,128)}, u32[]{:S(2)}) copy-start(s32[8,8,3]{1,0,2:T(8,128)} %param.11) | copy-start | bytes 2308
  3.4 33.5 %all-to-all-start.1 = ((bf16[32,128,128]{2,1,0:T(8,128)(2,1)}), bf16[32,128,128]{2,1,0:T(8,128)(2,1)S(1)}, u32[]{:S(2)}, u32[]{:S(2)}) async-start(bf16[32,128,128]{2,1,0:T(8,128)(2,1)} %shard_map.103), calls=%async_computation.1 | async-start | bytes 2097152 | tf_op jit(solution)/shard_map/all_to_all | solution.py:232
  36.9 1.0 copy-start.4
  37.9 55.3 %all-to-all-start = ((bf16[32,272,128]{2,1,0:T(8,128)(2,1)}), bf16[32,272,128]{2,1,0:T(8,128)(2,1)S(1)}, u32[]{:S(2)}, u32[]{:S(2)}) async-start(bf16[32,272,128]{2,1,0:T(8,128)(2,1)} %shard_map.102), calls=%async_computation | async-start | bytes 4456448 | tf_op jit(solution)/shard_map/all_to_all | solution.py:232
  41.5 56.6 %copy-start.7 = (s32[2]{0:T(128)S(1)}, s32[2]{0:T(128)}, u32[]{:S(2)}) copy-start(s32[2]{0:T(128)} %param.12) | copy-start | bytes 28
  93.2 5.8 %copy-start = (bf16[32,272,128]{2,1,0:T(8,128)(2,1)}, bf16[32,272,128]{2,1,0:T(8,128)(2,1)S(1)}, u32[]{:S(2)}) copy-start(bf16[32,272,128]{2,1,0:T(8,128)(2,1)S(1)} %all-to-all-done.kv_ref) | copy-start | bytes 6684676
  93.2 30.9 %all-to-all-start.3 = ((bf16[32,128,128]{2,1,0:T(8,128)(2,1)}), bf16[32,128,128]{2,1,0:T(8,128)(2,1)S(1)}, u32[]{:S(2)}, u32[]{:S(2)}) async-start(bf16[32,128,128]{2,1,0:T(8,128)(2,1)} %shard_map.105), calls=%async_computation.3 | async-start | bytes 2097152 | tf_op jit(solution)/shard_map/all_to_all | solution.py:232
  124.2 1.0 copy-start.3
  125.1 31.9 %all-to-all-start.2 = ((bf16[8,2,256,128]{3,2,1,0:T(8,128)(2,1)}), bf16[8,2,256,128]{3,2,1,0:T(8,128)(2,1)S(1)}, u32[]{:S(2)}, u32[]{:S(2)}) async-start(bf16[8,2,256,128]{3,2,1,0:T(8,128)(2,1)} %get-tuple-element.13), calls=%async_computation.2 | async-start | bytes 2097152 | tf_op jit(solution)/shard_map/all_to_all | solution.py:242
  157.0 31.4 %copy-start.2 = (bf16[8,2,256,128]{3,2,1,0:T(8,128)(2,1)}, bf16[8,2,256,128]{3,2,1,0:T(8,128)(2,1)S(1)}, u32[]{:S(2)}) copy-start(bf16[8,2,256,128]{3,2,1,0:T(8,128)(2,1)S(1)} %all-to-all-done.2.refs_0_) | copy-start | bytes 3145732
  188.5 51.4 %all-to-all-start.5 = ((bf16[8,2,512,128]{3,2,1,0:T(8,128)(2,1)}), bf16[8,2,512,128]{3,2,1,0:T(8,128)(2,1)S(1)}, u32[]{:S(2)}, u32[]{:S(2)}) async-start(bf16[8,2,512,128]{3,2,1,0:T(8,128)(2,1)} %get-tuple-element.19), calls=%async_computation.5 | async-start | bytes 4194304 | tf_op jit(solution)/shard_map/all_to_all | solution.py:242
  239.9 1.3 copy-start.1

commit v3 on v2

v3 whole, which is shorter than its diff:
```python
import functools
import math

import jax
import jax.numpy as jnp
from jax import lax
from jax.experimental import pallas as pl
from jax.experimental.pallas import tpu as pltpu
from jax.sharding import PartitionSpec as P

HEAD_WIDTH = 128
BLOCK_TOKENS = 64
R = 3
G = 2
SLOTS = 3 + G + R
WIDE = SLOTS * BLOCK_TOKENS
UNROLL = 4
VMEM_LIMIT = 56 * 1024 * 1024

keep_prob = 0.9

vmem = pl.BlockSpec(memory_space=pltpu.VMEM)
smem = pl.BlockSpec(memory_space=pltpu.SMEM)


def copy_cost(size):
    return pl.CostEstimate(flops=0, bytes_accessed=4 * size, transcendentals=0)


def block_rows(number):
    start = number * BLOCK_TOKENS
    if not isinstance(number, int):
        start = pl.multiple_of(start, BLOCK_TOKENS)
    return pl.ds(start, BLOCK_TOKENS)


def pack_kernel(heads, *refs):
    out_ref = refs[-1]
    begin = 0
    for ref in refs[:-1]:
        if len(ref.shape) == 3:
            rows = ref.shape[1]
            for m in range(heads):
                out_ref[m, 0, pl.ds(begin, rows), :] = ref[m]
        else:
            rows = ref.shape[0]
            for m in range(heads):
                out_ref[m, 0, pl.ds(begin, rows), :] = ref[:, pl.ds(m * HEAD_WIDTH, HEAD_WIDTH)]
        begin += rows


def pack(groups, heads, *sources):
    specs, arrays, total = [], [], 0
    for source in sources:
        if isinstance(source, tuple):
            array, at, rows = source
            specs.append(
                pl.BlockSpec((rows, heads * HEAD_WIDTH), functools.partial(lambda at, g: (at, g), at))
            )
        else:
            array, rows = source, source.shape[1]
            specs.append(pl.BlockSpec(source.shape, lambda g: (0, 0, 0)))
        arrays.append(array)
        total += rows
    shape = (heads, groups, total, HEAD_WIDTH)
    packed = pl.pallas_call(
        functools.partial(pack_kernel, heads),
        grid=(groups,),
        out_shape=jax.ShapeDtypeStruct(shape, jnp.bfloat16),
        in_specs=specs,
        out_specs=pl.BlockSpec((heads, 1, total, HEAD_WIDTH), lambda g: (0, g, 0, 0)),
        compiler_params=pltpu.CompilerParams(vmem_limit_bytes=VMEM_LIMIT),
        cost_estimate=copy_cost(math.prod(shape)),
    )(*arrays)
    return packed.reshape(heads * groups, total, HEAD_WIDTH)


def unpack_kernel(begins, step_heads, piece_ref, *refs):
    outs = refs[len(refs) - len(begins) :]
    for begin, out in zip(begins, outs):
        runs, _, rows, _ = out.shape
        for m in range(step_heads):
            for i in range(runs):
                out[i, 0, :, pl.ds(m * HEAD_WIDTH, HEAD_WIDTH)] = piece_ref[
                    m, pl.ds(begin + i * rows, rows), :
                ]


def unpack(received, parts):
    heads, total, _ = received.shape
    step_heads = 2 if heads % 2 == 0 else 1
    width = step_heads * HEAD_WIDTH
    shapes, out_specs, begins, olds, aliases = [], [], [], [], {}
    size = 0
    for n, (begin, rows, runs, pieces, piece, old) in enumerate(parts):
        begins.append(begin)
        shapes.append(
            jax.ShapeDtypeStruct((runs, pieces, rows, heads * HEAD_WIDTH), jnp.bfloat16)
        )
        out_specs.append(
            pl.BlockSpec(
                (runs, 1, rows, width), functools.partial(lambda piece, h: (0, piece, 0, h), piece)
            )
        )
        size += rows * runs * heads * HEAD_WIDTH
        if old is not None:
            aliases[1 + len(olds)] = n
            olds.append(old)
    return pl.pallas_call(
        functools.partial(unpack_kernel, begins, step_heads),
        grid=(heads // step_heads,),
        out_shape=shapes,
        in_specs=[pl.BlockSpec((step_heads, total, HEAD_WIDTH), lambda h: (h, 0, 0))]
        + [pl.BlockSpec(memory_space=pl.ANY)] * len(olds),
        out_specs=out_specs,
        input_output_aliases=aliases,
        compiler_params=pltpu.CompilerParams(vmem_limit_bytes=VMEM_LIMIT),
        cost_estimate=copy_cost(size),
    )(received, *olds)


def attention_kernel(
    last_block,
    device_blocks,
    per,
    piece,
    qd_begin,
    has_qd,
    has_start,
    is_last,
    joined,
    ids_ref,
    first_ref,
    drop_ref,
    kv_ref,
    *refs,
):
    refs = list(refs)
    qd_ref = refs.pop(0) if has_qd else kv_ref
    start_ref = refs.pop(0) if has_start else None
    out_ref = refs.pop(0)
    dkv_ref = None
    if is_last and not joined:
        dkv_ref = refs.pop(0)
    acc, retain = refs
    scale = HEAD_WIDTH ** (-0.5)
    steps = qd_ref.shape[0] * per
    slot_of_lane = lax.broadcasted_iota(jnp.int32, (SLOTS, WIDE), 1) // BLOCK_TOKENS
    slot_row = lax.broadcasted_iota(jnp.int32, (SLOTS, WIDE), 0)
    expand = (slot_of_lane == slot_row).astype(jnp.float32)
    retain[...] = jnp.dot(
        drop_ref[...].astype(jnp.float32), expand, preferred_element_type=jnp.float32
    ) * (1.0 / keep_prob)
    acc[...] = start_ref[...] if has_start else jnp.zeros_like(acc)
    lane = lax.broadcasted_iota(jnp.int32, (1, WIDE), 1)
    nt = (((1,), (1,)), ((), ()))
    tn = (((0,), (0,)), ((), ()))
    targets = out_ref.shape[0]
    out_steps = steps // targets
    out_rows = out_steps * BLOCK_TOKENS
    q_block = qd_begin // BLOCK_TOKENS

    def load(i):
        source, sub = i // per, i % per
        j = source * device_blocks + piece * per + sub
        ids = [ids_ref[j * SLOTS + s] for s in range(SLOTS)]
        qd_rows = [pl.ds(qd_begin, BLOCK_TOKENS), pl.ds(qd_begin + BLOCK_TOKENS, BLOCK_TOKENS)]
        if per > 1:
            qd_rows = [
                pl.ds(pl.multiple_of(qd_begin + (n * per + sub) * BLOCK_TOKENS, 16), BLOCK_TOKENS)
                for n in range(2)
            ]
        q = qd_ref[source, qd_rows[0], :]
        do = qd_ref[source, qd_rows[1], :]
        keys, vals = [
            jnp.concatenate(
                [
                    kv_ref[b // device_blocks, block_rows(n * device_blocks + b % device_blocks), :]
                    for b in ids
                ],
                axis=0,
            )
            for n in range(2)
        ]
        keep = retain[pl.ds(j, 1), :]
        return i, first_ref[0] + j, ids, q, do, keys, vals, keep

    def work(i, block_id, ids, q, do, keys, vals, keep):
        absent = ((block_id == 0) & (lane < BLOCK_TOKENS)) | (
            (block_id == last_block) & (lane >= 2 * BLOCK_TOKENS) & (lane < 3 * BLOCK_TOKENS)
        )
        logits = lax.dot_general(q, keys, nt, preferred_element_type=jnp.float32)
        raw = lax.dot_general(do, vals, nt, preferred_element_type=jnp.float32)
        logits = jnp.where(absent, -jnp.inf, logits)
        top = jnp.max(logits, axis=-1, keepdims=True)
        expd = jnp.exp2((logits - top) * (scale / math.log(2.0)))
        probs = expd * (1.0 / jnp.sum(expd, axis=-1, keepdims=True))
        kept = probs * keep
        weighted = kept * raw
        delta = jnp.sum(weighted, axis=-1, keepdims=True)
        dropped = kept.astype(jnp.bfloat16)
        dscores = (weighted - probs * delta).astype(jnp.bfloat16)
        att = jnp.dot(dropped, vals, preferred_element_type=jnp.float32)
        dq = jnp.dot(dscores, keys, preferred_element_type=jnp.float32) * scale
        none = jnp.zeros_like(q)
        terms = lax.dot_general(
            jnp.concatenate([dscores, dropped], axis=0),
            jnp.concatenate(
                [jnp.concatenate([q, none], axis=1), jnp.concatenate([none, do], axis=1)], axis=0
            ),
            tn,
            preferred_element_type=jnp.float32,
        )
        for s, b in enumerate(ids):
            acc[block_rows(b), :] += terms[s * BLOCK_TOKENS : (s + 1) * BLOCK_TOKENS]
        target, pos = i // out_steps, i % out_steps
        out_ref[target, block_rows(pos), :] = att.astype(jnp.bfloat16)
        out_ref[target, block_rows(out_steps + pos), :] = dq.astype(jnp.bfloat16)

    def step(t, carry):
        loaded = [load(t * UNROLL + u) for u in range(UNROLL)]
        for block in loaded:
            work(*block)
        return carry

    lax.fori_loop(0, steps // UNROLL, step, 0)
    if is_last:
        target_ref, begin = (out_ref, 2 * out_rows) if joined else (dkv_ref, 0)
        shards = target_ref.shape[0]
        rows = acc.shape[0] // shards
        for s in range(shards):
            part = pl.ds(s * rows, rows)
            target_ref[s, pl.ds(begin, rows), :] = (acc[part, :HEAD_WIDTH] * scale).astype(
                target_ref.dtype
            )
            target_ref[s, pl.ds(begin + rows, rows), :] = acc[part, HEAD_WIDTH:].astype(
                target_ref.dtype
            )


def attend(
    ids, first_block, drop, kv, qd, qd_begin, start, piece, per, is_last, device_blocks, total_blocks, shards, targets
):
    team_blocks = drop.shape[0]
    source = kv if qd is None else qd
    steps = source.shape[0] * per
    length = total_blocks * BLOCK_TOKENS
    pairs = steps * BLOCK_TOKENS * WIDE
    joined = shards == targets
    accumulator = (length, 2 * HEAD_WIDTH)
    out_rows = 2 * steps * BLOCK_TOKENS // targets
    grad_rows = 2 * length // shards
    out_shape = []
    scratch = [pltpu.VMEM((team_blocks, WIDE), jnp.float32)]
    if is_last:
        scratch = [pltpu.VMEM(accumulator, jnp.float32)] + scratch
        if joined:
            out_rows += grad_rows
        else:
            out_shape.append(jax.ShapeDtypeStruct((shards, grad_rows, HEAD_WIDTH), jnp.float32))
    else:
        out_shape.append(jax.ShapeDtypeStruct(accumulator, jnp.float32))
    out_shape.insert(0, jax.ShapeDtypeStruct((targets, out_rows, HEAD_WIDTH), jnp.bfloat16))
    operands = [kv] + [t for t in (qd, start) if t is not None]
    return pl.pallas_call(
        functools.partial(
            attention_kernel,
            total_blocks - 1,
            device_blocks,
            per,
            piece,
            qd_begin,
            qd is not None,
            start is not None,
            is_last,
            joined,
        ),
        out_shape=out_shape,
        in_specs=[smem, smem, vmem] + [vmem] * len(operands),
        out_specs=[vmem] * len(out_shape),
        scratch_shapes=scratch,
        compiler_params=pltpu.CompilerParams(vmem_limit_bytes=VMEM_LIMIT),
        cost_estimate=pl.CostEstimate(
            flops=12 * pairs * HEAD_WIDTH,
            bytes_accessed=2 * (source.size + kv.size) + 8 * length * HEAD_WIDTH,
            transcendentals=pairs,
        ),
    )(ids, first_block, drop, *operands)


def per_device(queries, keys, values, grad_out, rand_blocks, global_ids, drop_mask):
    shards = lax.axis_size("seq")
    groups = lax.axis_size("head")
    shard = lax.axis_index("seq")
    heads, shard_blocks, _ = rand_blocks.shape
    tokens = queries.shape[0]
    device_blocks = tokens // BLOCK_TOKENS
    shard_tokens = shard_blocks * BLOCK_TOKENS
    teams = shards // heads
    team = shard // heads
    team_blocks = heads * shard_blocks
    total_blocks = shards * shard_blocks
    first_block = team * team_blocks
    whole = teams == 1
    pieces = device_blocks if whole else 1
    per = device_blocks // pieces
    rows = tokens // pieces
    same_team = None if whole else [[t * heads + m for m in range(heads)] for t in range(teams)]
    same_team_all = (
        None
        if whole
        else [
            [(t * heads + m) * groups + g for m in range(heads) for g in range(groups)]
            for t in range(teams)
        ]
    )
    same_head = [[t * heads + m for t in range(teams)] for m in range(heads)]

    def to_heads(packed):
        return lax.all_to_all(
            packed,
            ("seq", "head"),
            split_axis=0,
            concat_axis=0,
            tiled=True,
            axis_index_groups=same_team_all,
        )

    def to_shards(results):
        return lax.all_to_all(
            results, "seq", split_axis=0, concat_axis=0, tiled=True, axis_index_groups=same_team
        )

    table_rows = -(-shard_blocks // 16) * 16
    tables = jnp.concatenate([rand_blocks, drop_mask], axis=2).astype(jnp.bfloat16)
    tables = jnp.pad(
        tables, ((0, 0), (0, table_rows - shard_blocks), (0, HEAD_WIDTH - R - SLOTS))
    )
    kv_sources = [(keys, 0, tokens), (values, 0, tokens), tables]
    qd_sources = [[(queries, c, rows), (grad_out, c, rows)] for c in range(pieces)]
    qd_begin = 2 * tokens + table_rows
    kv = to_heads(pack(groups, heads, *kv_sources, *qd_sources[0]))
    later = [to_heads(pack(groups, heads, *sources)) for sources in qd_sources[1:]]
    tables = lax.dynamic_index_in_dim(
        kv.reshape(heads, groups, -1, HEAD_WIDTH)[
            :, :, 2 * tokens : 2 * tokens + shard_blocks, : R + SLOTS
        ],
        lax.axis_index("head"),
        axis=1,
        keepdims=False,
    )
    tables = tables.reshape(team_blocks, R + SLOTS).astype(jnp.int32)
    qd = [None] + later
    if not whole:
        qd[0] = kv[:, qd_begin:]
        kv = lax.all_gather(kv[:, : 2 * tokens], "seq", axis=0, tiled=True, axis_index_groups=same_head)
    blocks = first_block + jnp.arange(team_blocks, dtype=jnp.int32)
    window = jnp.stack([blocks - 1, blocks, blocks + 1], axis=1)
    listed = jnp.concatenate(
        [window, jnp.broadcast_to(global_ids[None], (team_blocks, G)), tables[:, :R]], axis=1
    )
    listed = jnp.clip(listed, 0, total_blocks - 1).reshape(-1)
    near = []
    sums = None
    for c in range(pieces):
        result, *sums = attend(
            listed,
            first_block.reshape(1),
            tables[:, R:],
            kv,
            qd[c],
            qd_begin if qd[c] is None else 0,
            sums[0] if sums else None,
            c,
            per,
            c == pieces - 1,
            device_blocks,
            total_blocks,
            shards,
            heads,
        )
        near.append(to_shards(result))
    runs = shard_blocks // device_blocks
    att, dq = None, None
    for c in range(pieces):
        begin = shard_tokens // pieces
        parts = [(0, rows, runs, pieces, c, att), (begin, rows, runs, pieces, c, dq)]
        if c < pieces - 1:
            att, dq = unpack(near[c], parts)
        elif whole:
            grads = [(2 * begin + n * shard_tokens, shard_tokens, 1, 1, 0, None) for n in range(2)]
            att, dq, dk, dv = unpack(near[c], parts + grads)
        else:
            att, dq = unpack(near[c], parts)
            grads = lax.psum_scatter(
                sums[0], "seq", scatter_dimension=0, tiled=True, axis_index_groups=same_head
            ).astype(jnp.bfloat16)
            grads = to_shards(grads)
            dk, dv = unpack(
                grads, [(n * shard_tokens, shard_tokens, 1, 1, 0, None) for n in range(2)]
            )
    return tuple(t.reshape(shard_tokens, heads * HEAD_WIDTH) for t in (att, dq, dk, dv))


def solution(mesh):
    return jax.shard_map(
        per_device,
        mesh=mesh,
        in_specs=(
            P(("seq", "head"), None),
            P(("seq", "head"), None),
            P(("seq", "head"), None),
            P(("seq", "head"), None),
            P("head", "seq", None),
            P(),
            P("head", "seq", None),
        ),
        out_specs=(P("seq", "head"), P("seq", "head"), P("seq", "head"), P("seq", "head")),
        check_vma=False,
    )
```

time: 245 us -> 232 us (0.947)
  blocking collectives: 31.4 us -> 0 us
  waiting for transfers between devices: 116 us -> 141 us
  starting transfers between devices: 24.3 us -> 19.7 us
  Pallas kernels: 66.7 us -> 62.7 us
    all_to_all x1 -> x0, blocking collectives: 31.4 us -> none  [to_shards(): lax.all_to_all(results, 'seq', split_axis=0, concat_axis=0, tiled=True, a...]
    all_to_all x2, waiting for transfers between devices: 44.6 us -> 68.9 us  [to_shards(): lax.all_to_all(results, 'seq', split_axis=0, concat_axis=0, tiled=True, a...]
    pallas_call x2, Pallas kernels: 51 us -> 47.1 us  [attend(): pl.pallas_call(functools.partial(attention_kernel, total_blocks - 1, devi...]
    all_to_all x3 -> x2, starting transfers between devices: 14.9 us -> 11.4 us  [to_heads(): lax.all_to_all(packed, ('seq', 'head'), split_axis=0, concat_axis=0, tile...]
    all_to_all x3 -> x2, waiting for transfers between devices: 71 us -> 72.4 us  [to_heads(): lax.all_to_all(packed, ('seq', 'head'), split_axis=0, concat_axis=0, tile...]
    pallas_call x5 -> x4, Pallas kernels: 15.7 us -> 15.7 us  [the longest x2 7.9 us: pack(): pl.pallas_call(functools.partial(pack_kernel, heads), grid=(groups,), out...]
  transfers between devices with their start and end apart: 5 -> 4, of which waited for: 4 -> 4; matrix products, arithmetic and copies ran while one was open for 1% -> 1% of each run, Pallas kernels for 25% -> 23%
where the time goes in v3:
time: 232 us; the launch traced here: 231 us
  waiting for transfers between devices  141 us (61%)
  Pallas kernels  62.7 us (27%)
  starting transfers between devices  19.7 us (8%)
  local copies, waits for them, and re-layouts  4.39 us (2%)
    all_to_all x2, waiting for transfers between devices, to_heads(): lax.all_to_all(packed, ('seq', 'head'), split_axis=0, concat_axis=0, tile...  72.4 us
    all_to_all x2, waiting for transfers between devices, to_shards(): lax.all_to_all(results, 'seq', split_axis=0, concat_axis=0, tiled=True, a...  68.9 us
    pallas_call x2, Pallas kernels, attend(): pl.pallas_call(functools.partial(attention_kernel, total_blocks - 1, devi...  47.1 us
    all_to_all x2, starting transfers between devices, to_heads(): lax.all_to_all(packed, ('seq', 'head'), split_axis=0, concat_axis=0, tile...  11.4 us
    all_to_all x2, starting transfers between devices, to_shards(): lax.all_to_all(results, 'seq', split_axis=0, concat_axis=0, tiled=True, a...  8.28 us
    pallas_call x2, Pallas kernels, pack(): pl.pallas_call(functools.partial(pack_kernel, heads), grid=(groups,), out...  7.9 us
    pallas_call x2, Pallas kernels, unpack(): pl.pallas_call(functools.partial(unpack_kernel, begins, step_heads), grid...  7.76 us
  transfers between devices with their start and end apart: 4, of which 4 were waited for; matrix products, arithmetic and copies ran while one was open for 1% of the time, Pallas kernels for 23%

profile of v3, /device:TPU:0, one launch (start us, length us, event | category | flops | bytes accessed | tf_op | source)
XLA Modules:
  0.0 231.0 jit_solution(10235403905696560056)
XLA Ops:
  0.6 0.7 convert.7
  1.3 0.1 copy.18
  1.5 0.8 convert.8
  2.2 0.7 fusion.5.refs_2_
  2.9 4.4 %shard_map.102 = bf16[8,4,400,128]{3,2,1,0:T(8,128)(2,1)} custom-call(bf16[128,4096]{1,0:T(8,128)(2,1)} %refs_0_.2, bf16[128,4096]{1,0:T(8,128)(2,1)} %refs_1_.2, bf16[8,16,128]{2,1,0:T(8,128)(2,1)} %fusion.5.refs_2_, bf16[128,4096]{1,0:T(8,128)(2,1)} %refs_0_.3, bf16[128,4096]{1,0:T(8,128)(2,1)} %refs_1_.3), custom_call_target="tpu_custom_call" | custom-call | bytes 6553600 | tf_op jit(solution)/shard_map/pallas_call | solution.py:66
  7.4 7.3 %all-to-all-start = ((bf16[32,400,128]{2,1,0:T(8,128)(2,1)}), bf16[32,400,128]{2,1,0:T(8,128)(2,1)S(1)}, u32[]{:S(2)}, u32[]{:S(2)}) async-start(bf16[32,400,128]{2,1,0:T(8,128)(2,1)} %bitcast.13), calls=%async_computation | async-start | bytes 6553600 | tf_op jit(solution)/shard_map/all_to_all | solution.py:320
  14.7 0.0 copy-start.3
  14.7 3.5 %shard_map.103 = bf16[8,4,128,128]{3,2,1,0:T(8,128)(2,1)} custom-call(bf16[128,4096]{1,0:T(8,128)(2,1)} %refs_0_.3, bf16[128,4096]{1,0:T(8,128)(2,1)} %refs_1_.3), custom_call_target="tpu_custom_call" | custom-call | bytes 2097152 | tf_op jit(solution)/shard_map/pallas_call | solution.py:66
  18.2 70.8 %all-to-all-done.kv_ref = bf16[32,400,128]{2,1,0:T(8,128)(2,1)S(1)} async-done(((bf16[32,400,128]{2,1,0:T(8,128)(2,1)}), bf16[32,400,128]{2,1,0:T(8,128)(2,1)S(1)}, u32[]{:S(2)}, u32[]{:S(2)}) %all-to-all-start) | async-done | bytes 3276832 | tf_op jit(solution)/shard_map/all_to_all | solution.py:320
  88.9 0.0 copy-start
  88.9 4.1 %all-to-all-start.1 = ((bf16[32,128,128]{2,1,0:T(8,128)(2,1)}), bf16[32,128,128]{2,1,0:T(8,128)(2,1)}, u32[]{:S(2)}, u32[]{:S(2)}) async-start(bf16[32,128,128]{2,1,0:T(8,128)(2,1)} %bitcast.14), calls=%async_computation.1 | async-start | bytes 2097152 | tf_op jit(solution)/shard_map/all_to_all | solution.py:320
  93.1 0.7 slice.15.drop_ref
  93.8 0.1 copy.19
  93.9 0.0 copy-done.3
  93.9 0.1 broadcast_in_dim.2
  94.0 0.1 copy.20
  94.1 0.7 min.12.ids_ref
  94.7 0.0 copy-done
  94.7 22.9 %shard_map.104 = (bf16[8,512,128]{2,1,0:T(8,128)(2,1)}, f32[4096,256]{1,0:T(8,128)}) custom-call(s32[512]{0:T(512)} %min.12.ids_ref, s32[1]{0:T(128)} %bitcast.3.first_ref, s32[64,8]{1,0:T(8,128)} %slice.15.drop_ref, bf16[32,400,128]{2,1,0:T(8,128)(2,1)} %copy-done), custom_call_target="tpu_custom_call" | custom-call | flops 1610612736 | bytes 10747904 | tf_op jit(solution)/shard_map/pallas_call | solution.py:265
  117.6 1.6 all-to-all-done.1.refs_0_
  119.2 4.1 %all-to-all-start.3 = ((bf16[8,512,128]{2,1,0:T(8,128)(2,1)}), bf16[8,512,128]{2,1,0:T(8,128)(2,1)S(1)}, u32[]{:S(2)}, u32[]{:S(2)}) async-start(bf16[8,512,128]{2,1,0:T(8,128)(2,1)} %get-tuple-element.13), calls=%async_computation.3 | async-start | bytes 2097152 | tf_op jit(solution)/shard_map/all_to_all | solution.py:330
  123.4 24.2 %shard_map.105 = bf16[8,1536,128]{2,1,0:T(8,128)(2,1)} custom-call(s32[512]{0:T(512)} %min.12.ids_ref, s32[1]{0:T(128)} %bitcast.3.first_ref, s32[64,8]{1,0:T(8,128)} %slice.15.drop_ref, bf16[32,400,128]{2,1,0:T(8,128)(2,1)} %copy-done, bf16[32,128,128]{2,1,0:T(8,128)(2,1)} %all-to-all-done.1.refs_0_, f32[4096,256]{1,0:T(8,128)} %get-tuple-element.12.refs_1_), custom_call_target="tpu_custom_call" | custom-call | flops 1610612736 | bytes 8519680 | tf_op jit(solution)/shard_map/pallas_call | solution.py:265
  147.6 1.9 all-to-all-done.3.piece_ref
  149.5 0.0 copy-start.2
  149.5 1.0 copy-done.2
  150.4 4.1 %all-to-all-start.2 = ((bf16[8,1536,128]{2,1,0:T(8,128)(2,1)}), bf16[8,1536,128]{2,1,0:T(8,128)(2,1)S(1)}, u32[]{:S(2)}, u32[]{:S(2)}) async-start(bf16[8,1536,128]{2,1,0:T(8,128)(2,1)} %shard_map.105), calls=%async_computation.2 | async-start | bytes 6291456 | tf_op jit(solution)/shard_map/all_to_all | solution.py:330
  154.6 3.4 %shard_map.106 = (bf16[4,2,64,1024]{3,2,1,0:T(8,128)(2,1)}, bf16[4,2,64,1024]{3,2,1,0:T(8,128)(2,1)}) custom-call(bf16[8,512,128]{2,1,0:T(8,128)(2,1)} %copy-done.2), custom_call_target="tpu_custom_call" | custom-call | bytes 2097152 | tf_op jit(solution)/shard_map/pallas_call | solution.py:109
  158.0 67.1 %all-to-all-done.2.piece_ref = bf16[8,1536,128]{2,1,0:T(8,128)(2,1)S(1)} async-done(((bf16[8,1536,128]{2,1,0:T(8,128)(2,1)}), bf16[8,1536,128]{2,1,0:T(8,128)(2,1)S(1)}, u32[]{:S(2)}, u32[]{:S(2)}) %all-to-all-start.2) | async-done | bytes 3145760 | tf_op jit(solution)/shard_map/all_to_all | solution.py:330
  225.0 0.0 copy-start.1
  225.0 1.6 copy-done.1
  226.7 4.3 %shard_map.107 = (bf16[4,2,64,1024]{3,2,1,0:T(8,128)(2,1)}, bf16[4,2,64,1024]{3,2,1,0:T(8,128)(2,1)}, bf16[1,1,512,1024]{3,2,1,0:T(8,128)(2,1)}, bf16[1,1,512,1024]{3,2,1,0:T(8,128)(2,1)}) custom-call(bf16[8,1536,128]{2,1,0:T(8,128)(2,1)} %copy-done.1, ...), custom_call_target="tpu_custom_call", output_to_operand_aliasing={{0}: (1, {}), {1}: (2, {})} | custom-call | bytes 6291456 | tf_op jit(solution)/shard_map/pallas_call | solution.py:109
  (6 shorter events, 0.1 us)
Async XLA Ops:
  7.4 81.6 %all-to-all-start = ((bf16[32,400,128]{2,1,0:T(8,128)(2,1)}), bf16[32,400,128]{2,1,0:T(8,128)(2,1)S(1)}, u32[]{:S(2)}, u32[]{:S(2)}) async-start(bf16[32,400,128]{2,1,0:T(8,128)(2,1)} %bitcast.13), calls=%async_computation | async-start | bytes 6553600 | tf_op jit(solution)/shard_map/all_to_all | solution.py:320
  14.7 79.2 %copy-start.3 = (s32[2]{0:T(128)S(1)}, s32[2]{0:T(128)}, u32[]{:S(2)}) copy-start(s32[2]{0:T(128)} %param.12) | copy-start | bytes 28
  88.9 5.8 %copy-start = (bf16[32,400,128]{2,1,0:T(8,128)(2,1)}, bf16[32,400,128]{2,1,0:T(8,128)(2,1)S(1)}, u32[]{:S(2)}) copy-start(bf16[32,400,128]{2,1,0:T(8,128)(2,1)S(1)} %all-to-all-done.kv_ref) | copy-start | bytes 9830404
  88.9 30.3 %all-to-all-start.1 = ((bf16[32,128,128]{2,1,0:T(8,128)(2,1)}), bf16[32,128,128]{2,1,0:T(8,128)(2,1)}, u32[]{:S(2)}, u32[]{:S(2)}) async-start(bf16[32,128,128]{2,1,0:T(8,128)(2,1)} %bitcast.14), calls=%async_computation.1 | async-start | bytes 2097152 | tf_op jit(solution)/shard_map/all_to_all | solution.py:320
  119.2 30.2 %all-to-all-start.3 = ((bf16[8,512,128]{2,1,0:T(8,128)(2,1)}), bf16[8,512,128]{2,1,0:T(8,128)(2,1)S(1)}, u32[]{:S(2)}, u32[]{:S(2)}) async-start(bf16[8,512,128]{2,1,0:T(8,128)(2,1)} %get-tuple-element.13), calls=%async_computation.3 | async-start | bytes 2097152 | tf_op jit(solution)/shard_map/all_to_all | solution.py:330
  149.5 1.0 copy-start.2
  150.4 74.6 %all-to-all-start.2 = ((bf16[8,1536,128]{2,1,0:T(8,128)(2,1)}), bf16[8,1536,128]{2,1,0:T(8,128)(2,1)S(1)}, u32[]{:S(2)}, u32[]{:S(2)}) async-start(bf16[8,1536,128]{2,1,0:T(8,128)(2,1)} %shard_map.105), calls=%async_computation.2 | async-start | bytes 6291456 | tf_op jit(solution)/shard_map/all_to_all | solution.py:330
  225.0 1.6 copy-start.1

commit v4 on v3

--- a/solution.py
+++ b/solution.py
@@ -124,12 +124,16 @@
     device_blocks,
     per,
     piece,
+    out_rows,
+    source_rows,
+    qd_rows,
     qd_begin,
     has_qd,
     has_start,
-    is_last,
     joined,
+    tokens,
     ids_ref,
+    starts_ref,
     first_ref,
     drop_ref,
     kv_ref,
@@ -139,12 +143,9 @@
     qd_ref = refs.pop(0) if has_qd else kv_ref
     start_ref = refs.pop(0) if has_start else None
     out_ref = refs.pop(0)
-    dkv_ref = None
-    if is_last and not joined:
-        dkv_ref = refs.pop(0)
-    acc, retain = refs
+    acc, retain, flipped = refs
     scale = HEAD_WIDTH ** (-0.5)
-    steps = qd_ref.shape[0] * per
+    steps = out_ref.shape[0] * (out_rows // BLOCK_TOKENS)
     slot_of_lane = lax.broadcasted_iota(jnp.int32, (SLOTS, WIDE), 1) // BLOCK_TOKENS
     slot_row = lax.broadcasted_iota(jnp.int32, (SLOTS, WIDE), 0)
     expand = (slot_of_lane == slot_row).astype(jnp.float32)
@@ -153,44 +154,75 @@
     ) * (1.0 / keep_prob)
     acc[...] = start_ref[...] if has_start else jnp.zeros_like(acc)
     lane = lax.broadcasted_iota(jnp.int32, (1, WIDE), 1)
-    nt = (((1,), (1,)), ((), ()))
+    low_half = lax.broadcasted_iota(jnp.int32, (HEAD_WIDTH, 2 * BLOCK_TOKENS), 1) < BLOCK_TOKENS
     tn = (((0,), (0,)), ((), ()))
     targets = out_ref.shape[0]
     out_steps = steps // targets
-    out_rows = out_steps * BLOCK_TOKENS
-    q_block = qd_begin // BLOCK_TOKENS
+
+    def flip(i, carry):
+        for n in range(2):
+            pair = [
+                kv_ref[
+                    pl.ds(
+                        pl.multiple_of(i * source_rows + n * tokens + h * BLOCK_TOKENS, 16),
+                        BLOCK_TOKENS,
+                    ),
+                    :,
+                ]
+                for h in range(2)
+            ]
+            flipped[n, 2 * i] = jnp.concatenate(pair, axis=0).T
+            flipped[n, 2 * i + 1] = jnp.concatenate(pair[::-1], axis=0).T
+        return carry
+
+    lax.fori_loop(0, flipped.shape[1] // 2, flip, 0)
 
     def load(i):
-        source, sub = i // per, i % per
+        if per == 1:
+            source, sub = i, 0
+        else:
+            source, sub = lax.div(i, per), lax.rem(i, per)
         j = source * device_blocks + piece * per + sub
         ids = [ids_ref[j * SLOTS + s] for s in range(SLOTS)]
-        qd_rows = [pl.ds(qd_begin, BLOCK_TOKENS), pl.ds(qd_begin + BLOCK_TOKENS, BLOCK_TOKENS)]
-        if per > 1:
-            qd_rows = [
-                pl.ds(pl.multiple_of(qd_begin + (n * per + sub) * BLOCK_TOKENS, 16), BLOCK_TOKENS)
-                for n in range(2)
+        starts = [starts_ref[j * SLOTS + s] for s in range(SLOTS)]
+        q, do = [
+            qd_ref[
+                pl.ds(
+                    pl.multiple_of(
+                        source * qd_rows + (n * per + sub) * BLOCK_TOKENS + qd_begin, 16
+                    ),
+                    BLOCK_TOKENS,
+                ),
+                :,
             ]
-        q = qd_ref[source, qd_rows[0], :]
-        do = qd_ref[source, qd_rows[1], :]
+            for n in range(2)
+        ]
         keys, vals = [
             jnp.concatenate(
+                [kv_ref[pl.ds(pl.multiple_of(r + n * tokens, 16), BLOCK_TOKENS), :] for r in starts],
+                axis=0,
+            )
+            for n in range(2)
+        ]
+        keys_t, vals_t = [
+            jnp.concatenate(
                 [
-                    kv_ref[b // device_blocks, block_rows(n * device_blocks + b % device_blocks), :]
-                    for b in ids
+                    jnp.where(low_half, flipped[n, ids[s]], flipped[n, ids[s + 1] ^ 1])
+                    for s in range(0, SLOTS, 2)
                 ],
-                axis=0,
+                axis=1,
             )
             for n in range(2)
         ]
         keep = retain[pl.ds(j, 1), :]
-        return i, first_ref[0] + j, ids, q, do, keys, vals, keep
-
-    def work(i, block_id, ids, q, do, keys, vals, keep):
+        return i, first_ref[0] + j, ids, q, do, keys, vals, keys_t, vals_t, keep
+
+    def work(i, block_id, ids, q, do, keys, vals, keys_t, vals_t, keep):
         absent = ((block_id == 0) & (lane < BLOCK_TOKENS)) | (
             (block_id == last_block) & (lane >= 2 * BLOCK_TOKENS) & (lane < 3 * BLOCK_TOKENS)
         )
-        logits = lax.dot_general(q, keys, nt, preferred_element_type=jnp.float32)
-        raw = lax.dot_general(do, vals, nt, preferred_element_type=jnp.float32)
+        logits = jnp.dot(q, keys_t, preferred_element_type=jnp.float32)
+        raw = jnp.dot(do, vals_t, preferred_element_type=jnp.float32)
         logits = jnp.where(absent, -jnp.inf, logits)
         top = jnp.max(logits, axis=-1, keepdims=True)
         expd = jnp.exp2((logits - top) * (scale / math.log(2.0)))
@@ -213,7 +245,7 @@
         )
         for s, b in enumerate(ids):
             acc[block_rows(b), :] += terms[s * BLOCK_TOKENS : (s + 1) * BLOCK_TOKENS]
-        target, pos = i // out_steps, i % out_steps
+        target, pos = lax.div(i, out_steps), lax.rem(i, out_steps)
         out_ref[target, block_rows(pos), :] = att.astype(jnp.bfloat16)
         out_ref[target, block_rows(out_steps + pos), :] = dq.astype(jnp.bfloat16)
 
@@ -224,44 +256,40 @@
         return carry
 
     lax.fori_loop(0, steps // UNROLL, step, 0)
-    if is_last:
-        target_ref, begin = (out_ref, 2 * out_rows) if joined else (dkv_ref, 0)
-        shards = target_ref.shape[0]
-        rows = acc.shape[0] // shards
-        for s in range(shards):
+    if joined:
+        rows = acc.shape[0] // targets
+        for s in range(targets):
             part = pl.ds(s * rows, rows)
-            target_ref[s, pl.ds(begin, rows), :] = (acc[part, :HEAD_WIDTH] * scale).astype(
-                target_ref.dtype
-            )
-            target_ref[s, pl.ds(begin + rows, rows), :] = acc[part, HEAD_WIDTH:].astype(
-                target_ref.dtype
+            out_ref[s, pl.ds(2 * out_rows, rows), :] = (acc[part, :HEAD_WIDTH] * scale).astype(
+                jnp.bfloat16
+            )
+            out_ref[s, pl.ds(2 * out_rows + rows, rows), :] = acc[part, HEAD_WIDTH:].astype(
+                jnp.bfloat16
             )
 
 
 def attend(
-    ids, first_block, drop, kv, qd, qd_begin, start, piece, per, is_last, device_blocks, total_blocks, shards, targets
+    ids, starts, first_block, drop, kv, qd, qd_begin, start, piece, per, joined, device_blocks, total_blocks, tokens, targets
 ):
     team_blocks = drop.shape[0]
     source = kv if qd is None else qd
-    steps = source.shape[0] * per
+    steps = team_blocks * per // device_blocks
     length = total_blocks * BLOCK_TOKENS
     pairs = steps * BLOCK_TOKENS * WIDE
-    joined = shards == targets
     accumulator = (length, 2 * HEAD_WIDTH)
-    out_rows = 2 * steps * BLOCK_TOKENS // targets
-    grad_rows = 2 * length // shards
-    out_shape = []
-    scratch = [pltpu.VMEM((team_blocks, WIDE), jnp.float32)]
-    if is_last:
+    out_rows = steps * BLOCK_TOKENS // targets
+    total_rows = 2 * out_rows + (2 * length // targets if joined else 0)
+    out_shape = [jax.ShapeDtypeStruct((targets, total_rows, HEAD_WIDTH), jnp.bfloat16)]
+    scratch = [
+        pltpu.VMEM((team_blocks, WIDE), jnp.float32),
+        pltpu.VMEM((2, total_blocks, HEAD_WIDTH, 2 * BLOCK_TOKENS), jnp.bfloat16),
+    ]
+    if joined:
         scratch = [pltpu.VMEM(accumulator, jnp.float32)] + scratch
-        if joined:
-            out_rows += grad_rows
-        else:
-            out_shape.append(jax.ShapeDtypeStruct((shards, grad_rows, HEAD_WIDTH), jnp.float32))
     else:
         out_shape.append(jax.ShapeDtypeStruct(accumulator, jnp.float32))
-    out_shape.insert(0, jax.ShapeDtypeStruct((targets, out_rows, HEAD_WIDTH), jnp.bfloat16))
-    operands = [kv] + [t for t in (qd, start) if t is not None]
+    flat = [t.reshape(-1, HEAD_WIDTH) for t in (kv, qd) if t is not None]
+    operands = flat + ([] if start is None else [start])
     return pl.pallas_call(
         functools.partial(
             attention_kernel,
@@ -269,14 +297,17 @@
             device_blocks,
             per,
             piece,
+            out_rows,
+            kv.shape[1],
+            source.shape[1],
             qd_begin,
             qd is not None,
             start is not None,
-            is_last,
             joined,
+            tokens,
         ),
         out_shape=out_shape,
-        in_specs=[smem, smem, vmem] + [vmem] * len(operands),
+        in_specs=[smem, smem, smem, vmem] + [vmem] * len(operands),
         out_specs=[vmem] * len(out_shape),
         scratch_shapes=scratch,
         compiler_params=pltpu.CompilerParams(vmem_limit_bytes=VMEM_LIMIT),
@@ -285,7 +316,7 @@
             bytes_accessed=2 * (source.size + kv.size) + 8 * length * HEAD_WIDTH,
             transcendentals=pairs,
         ),
-    )(ids, first_block, drop, *operands)
+    )(ids, starts, first_block, drop, *operands)
 
 
 def per_device(queries, keys, values, grad_out, rand_blocks, global_ids, drop_mask):
@@ -360,11 +391,13 @@
         [window, jnp.broadcast_to(global_ids[None], (team_blocks, G)), tables[:, :R]], axis=1
     )
     listed = jnp.clip(listed, 0, total_blocks - 1).reshape(-1)
+    starts = listed // device_blocks * kv.shape[1] + listed % device_blocks * BLOCK_TOKENS
     near = []
     sums = None
     for c in range(pieces):
         result, *sums = attend(
             listed,
+            starts,
             first_block.reshape(1),
             tables[:, R:],
             kv,
@@ -373,10 +406,10 @@
             sums[0] if sums else None,
             c,
             per,
-            c == pieces - 1,
+            whole and c == pieces - 1,
             device_blocks,
             total_blocks,
-            shards,
+            tokens,
             heads,
         )
         near.append(to_shards(result))
@@ -394,6 +427,9 @@
             att, dq = unpack(near[c], parts)
             grads = lax.psum_scatter(
                 sums[0], "seq", scatter_dimension=0, tiled=True, axis_index_groups=same_head
+            ).reshape(heads, shard_tokens, 2, HEAD_WIDTH)
+            grads = jnp.concatenate(
+                [grads[:, :, 0] * HEAD_WIDTH ** (-0.5), grads[:, :, 1]], axis=1
             ).astype(jnp.bfloat16)
             grads = to_shards(grads)
             dk, dv = unpack(

time: 232 us -> 235 us (1.013)
  Pallas kernels: 62.7 us -> 66.2 us
  starting transfers between devices: 19.7 us -> 23.1 us
  waiting for transfers between devices: 141 us -> 138 us
    pallas_call x2, Pallas kernels: 47.1 us -> 50.6 us  [attend(): pl.pallas_call(functools.partial(attention_kernel, total_blocks - 1, devi...]
    all_to_all x2, starting transfers between devices: 8.28 us -> 11.7 us  [to_shards(): lax.all_to_all(results, 'seq', split_axis=0, concat_axis=0, tiled=True, a...]
  transfers between devices with their start and end apart: 4 -> 4, of which waited for: 4 -> 3; matrix products, arithmetic and copies ran while one was open for 1% -> 1% of each run, Pallas kernels for 23% -> 25%
where the time goes in v4:
time: 235 us
  waiting for transfers between devices  138 us (59%)
  Pallas kernels  66.2 us (28%)
  starting transfers between devices  23.1 us (10%)
  local copies, waits for them, and re-layouts  3.83 us (2%)
  other arithmetic  2.81 us (1%)
    all_to_all x2, waiting for transfers between devices, to_heads(): lax.all_to_all(packed, ('seq', 'head'), split_axis=0, concat_axis=0, tile...  70.8 us
    all_to_all x2, waiting for transfers between devices, to_shards(): lax.all_to_all(results, 'seq', split_axis=0, concat_axis=0, tiled=True, a...  67.1 us
    pallas_call x2, Pallas kernels, attend(): pl.pallas_call(functools.partial(attention_kernel, total_blocks - 1, devi...  50.6 us
    all_to_all x2, starting transfers between devices, to_shards(): lax.all_to_all(results, 'seq', split_axis=0, concat_axis=0, tiled=True, a...  11.7 us
    all_to_all x2, starting transfers between devices, to_heads(): lax.all_to_all(packed, ('seq', 'head'), split_axis=0, concat_axis=0, tile...  11.4 us
    pallas_call x2, Pallas kernels, pack(): pl.pallas_call(functools.partial(pack_kernel, heads), grid=(groups,), out...  7.83 us
    pallas_call x2, Pallas kernels, unpack(): pl.pallas_call(functools.partial(unpack_kernel, begins, step_heads), grid...  7.76 us
  transfers between devices with their start and end apart: 4, of which 3 were waited for; matrix products, arithmetic and copies ran while one was open for 1% of the time, Pallas kernels for 25%

profile of v4, /device:TPU:0, one launch (start us, length us, event | category | flops | bytes accessed | tf_op | source)
XLA Modules:
  0.0 234.5 jit_solution(5772320801777034579)
XLA Ops:
  0.6 0.7 convert.7
  1.3 0.1 copy.21
  1.5 0.8 convert.8
  2.2 0.7 fusion.5.refs_2_
  2.9 4.4 %shard_map.102 = bf16[8,4,400,128]{3,2,1,0:T(8,128)(2,1)} custom-call(bf16[128,4096]{1,0:T(8,128)(2,1)} %refs_0_.2, bf16[128,4096]{1,0:T(8,128)(2,1)} %refs_1_.2, bf16[8,16,128]{2,1,0:T(8,128)(2,1)} %fusion.5.refs_2_, bf16[128,4096]{1,0:T(8,128)(2,1)} %refs_0_.3, bf16[128,4096]{1,0:T(8,128)(2,1)} %refs_1_.3), custom_call_target="tpu_custom_call" | custom-call | bytes 6553600 | tf_op jit(solution)/shard_map/pallas_call | solution.py:66
  7.3 7.3 %all-to-all-start = ((bf16[32,400,128]{2,1,0:T(8,128)(2,1)}), bf16[32,400,128]{2,1,0:T(8,128)(2,1)S(1)}, u32[]{:S(2)}, u32[]{:S(2)}) async-start(bf16[32,400,128]{2,1,0:T(8,128)(2,1)} %bitcast.19), calls=%async_computation | async-start | bytes 6553600 | tf_op jit(solution)/shard_map/all_to_all | solution.py:351
  14.6 0.0 copy-start.4
  14.6 3.5 %shard_map.103 = bf16[8,4,128,128]{3,2,1,0:T(8,128)(2,1)} custom-call(bf16[128,4096]{1,0:T(8,128)(2,1)} %refs_0_.3, bf16[128,4096]{1,0:T(8,128)(2,1)} %refs_1_.3), custom_call_target="tpu_custom_call" | custom-call | bytes 2097152 | tf_op jit(solution)/shard_map/pallas_call | solution.py:66
  18.1 70.8 %all-to-all-done = bf16[32,400,128]{2,1,0:T(8,128)(2,1)S(1)} async-done(((bf16[32,400,128]{2,1,0:T(8,128)(2,1)}), bf16[32,400,128]{2,1,0:T(8,128)(2,1)S(1)}, u32[]{:S(2)}, u32[]{:S(2)}) %all-to-all-start) | async-done | bytes 3276832 | tf_op jit(solution)/shard_map/all_to_all | solution.py:351
  88.9 0.0 copy-start
  88.9 4.1 %all-to-all-start.1 = ((bf16[32,128,128]{2,1,0:T(8,128)(2,1)}), bf16[32,128,128]{2,1,0:T(8,128)(2,1)}, u32[]{:S(2)}, u32[]{:S(2)}) async-start(bf16[32,128,128]{2,1,0:T(8,128)(2,1)} %bitcast.20), calls=%async_computation.1 | async-start | bytes 2097152 | tf_op jit(solution)/shard_map/all_to_all | solution.py:351
  93.0 0.7 slice.15.drop_ref
  93.7 0.1 copy.23
  93.8 0.0 copy-done.4
  93.8 0.1 broadcast_in_dim.2
  93.9 0.1 copy.24
  94.0 0.1 min.12.ids_ref
  94.1 0.0 copy-start.3
  94.1 0.6 fusion.7.starts_ref
  94.7 0.0 copy-done
  94.7 0.0 copy-done.3
  94.7 24.6 %shard_map.104 = (bf16[8,512,128]{2,1,0:T(8,128)(2,1)}, f32[4096,256]{1,0:T(8,128)}) custom-call(s32[512]{0:T(512)} %copy-done.3, s32[512]{0:T(512)} %fusion.7.starts_ref, s32[1]{0:T(128)} %bitcast.3.first_ref, s32[64,8]{1,0:T(8,128)} %slice.15.drop_ref, bf16[12800,128]{1,0:T(8,128)(2,1)} %bitcast.17), custom_call_target="tpu_custom_call" | custom-call | flops 1610612736 | bytes 10747904 | tf_op jit(solution)/shard_map/pallas_call | solution.py:293
  119.3 0.0 all-to-all-done.1
  119.3 5.8 %all-to-all-start.3 = ((bf16[8,512,128]{2,1,0:T(8,128)(2,1)}), bf16[8,512,128]{2,1,0:T(8,128)(2,1)S(1)}, u32[]{:S(2)}, u32[]{:S(2)}) async-start(bf16[8,512,128]{2,1,0:T(8,128)(2,1)} %get-tuple-element.13), calls=%async_computation.3 | async-start | bytes 2097152 | tf_op jit(solution)/shard_map/all_to_all | solution.py:361
  125.1 26.0 %shard_map.105 = bf16[8,1536,128]{2,1,0:T(8,128)(2,1)} custom-call(s32[512]{0:T(512)} %copy-done.3, s32[512]{0:T(512)} %fusion.7.starts_ref, s32[1]{0:T(128)} %bitcast.3.first_ref, s32[64,8]{1,0:T(8,128)} %slice.15.drop_ref, bf16[12800,128]{1,0:T(8,128)(2,1)} %bitcast.18, bf16[4096,128]{1,0:T(8,128)(2,1)} %bitcast.7.refs_0_, ...), custom_call_target="tpu_custom_call" | custom-call | flops 1610612736 | bytes 8519680 | tf_op jit(solution)/shard_map/pallas_call | solution.py:293
  151.1 0.1 all-to-all-done.3.piece_ref
  151.2 0.0 copy-start.2
  151.2 1.0 copy-done.2
  152.1 5.9 %all-to-all-start.2 = ((bf16[8,1536,128]{2,1,0:T(8,128)(2,1)}), bf16[8,1536,128]{2,1,0:T(8,128)(2,1)S(1)}, u32[]{:S(2)}, u32[]{:S(2)}) async-start(bf16[8,1536,128]{2,1,0:T(8,128)(2,1)} %shard_map.105), calls=%async_computation.2 | async-start | bytes 6291456 | tf_op jit(solution)/shard_map/all_to_all | solution.py:361
  158.1 3.4 %shard_map.106 = (bf16[4,2,64,1024]{3,2,1,0:T(8,128)(2,1)}, bf16[4,2,64,1024]{3,2,1,0:T(8,128)(2,1)}) custom-call(bf16[8,512,128]{2,1,0:T(8,128)(2,1)} %copy-done.2), custom_call_target="tpu_custom_call" | custom-call | bytes 2097152 | tf_op jit(solution)/shard_map/pallas_call | solution.py:109
  161.5 67.0 %all-to-all-done.2.piece_ref = bf16[8,1536,128]{2,1,0:T(8,128)(2,1)S(1)} async-done(((bf16[8,1536,128]{2,1,0:T(8,128)(2,1)}), bf16[8,1536,128]{2,1,0:T(8,128)(2,1)S(1)}, u32[]{:S(2)}, u32[]{:S(2)}) %all-to-all-start.2) | async-done | bytes 3145760 | tf_op jit(solution)/shard_map/all_to_all | solution.py:361
  228.5 0.0 copy-start.1
  228.5 1.7 copy-done.1
  230.2 4.3 %shard_map.107 = (bf16[4,2,64,1024]{3,2,1,0:T(8,128)(2,1)}, bf16[4,2,64,1024]{3,2,1,0:T(8,128)(2,1)}, bf16[1,1,512,1024]{3,2,1,0:T(8,128)(2,1)}, bf16[1,1,512,1024]{3,2,1,0:T(8,128)(2,1)}) custom-call(bf16[8,1536,128]{2,1,0:T(8,128)(2,1)} %copy-done.1, ...), custom_call_target="tpu_custom_call", output_to_operand_aliasing={{0}: (1, {}), {1}: (2, {})} | custom-call | bytes 6291456 | tf_op jit(solution)/shard_map/pallas_call | solution.py:109
  (6 shorter events, 0.1 us)
Async XLA Ops:
  7.3 81.6 %all-to-all-start = ((bf16[32,400,128]{2,1,0:T(8,128)(2,1)}), bf16[32,400,128]{2,1,0:T(8,128)(2,1)S(1)}, u32[]{:S(2)}, u32[]{:S(2)}) async-start(bf16[32,400,128]{2,1,0:T(8,128)(2,1)} %bitcast.19), calls=%async_computation | async-start | bytes 6553600 | tf_op jit(solution)/shard_map/all_to_all | solution.py:351
  14.6 79.2 %copy-start.4 = (s32[2]{0:T(128)S(1)}, s32[2]{0:T(128)}, u32[]{:S(2)}) copy-start(s32[2]{0:T(128)} %param.12) | copy-start | bytes 28
  88.9 5.8 %copy-start = (bf16[32,400,128]{2,1,0:T(8,128)(2,1)}, bf16[32,400,128]{2,1,0:T(8,128)(2,1)S(1)}, u32[]{:S(2)}) copy-start(bf16[32,400,128]{2,1,0:T(8,128)(2,1)S(1)} %all-to-all-done) | copy-start | bytes 9830404
  88.9 30.5 %all-to-all-start.1 = ((bf16[32,128,128]{2,1,0:T(8,128)(2,1)}), bf16[32,128,128]{2,1,0:T(8,128)(2,1)}, u32[]{:S(2)}, u32[]{:S(2)}) async-start(bf16[32,128,128]{2,1,0:T(8,128)(2,1)} %bitcast.20), calls=%async_computation.1 | async-start | bytes 2097152 | tf_op jit(solution)/shard_map/all_to_all | solution.py:351
  94.1 0.6 copy-start.3
  119.3 31.8 %all-to-all-start.3 = ((bf16[8,512,128]{2,1,0:T(8,128)(2,1)}), bf16[8,512,128]{2,1,0:T(8,128)(2,1)S(1)}, u32[]{:S(2)}, u32[]{:S(2)}) async-start(bf16[8,512,128]{2,1,0:T(8,128)(2,1)} %get-tuple-element.13), calls=%async_computation.3 | async-start | bytes 2097152 | tf_op jit(solution)/shard_map/all_to_all | solution.py:361
  151.2 1.0 copy-start.2
  152.1 76.4 %all-to-all-start.2 = ((bf16[8,1536,128]{2,1,0:T(8,128)(2,1)}), bf16[8,1536,128]{2,1,0:T(8,128)(2,1)S(1)}, u32[]{:S(2)}, u32[]{:S(2)}) async-start(bf16[8,1536,128]{2,1,0:T(8,128)(2,1)} %shard_map.105), calls=%async_computation.2 | async-start | bytes 6291456 | tf_op jit(solution)/shard_map/all_to_all | solution.py:361
  228.5 1.7 copy-start.1
